TPU v7x, 32 devices: a whole 2x2x4 slice. The times are simulated.
32 devices in a mesh: group: 2 (over y), patch: 4 (over z), head: 2 (over x), cfg: 2 (over core).
Axes of the slice: x: 2, y: 2, z: 4, core: 2. Of those that a mesh axis runs over, the one named last changes fastest.
Arguments:
- fresh_query: bfloat16 [4, 256, 2560], P(('group', 'cfg'), ('patch', 'head')), parts along dimension 0, may hold values from -32 to 32
- fresh_key: bfloat16 [4, 256, 2560], P(('group', 'cfg'), ('patch', 'head')), parts along dimension 0, may hold values from -9 to 9
- fresh_value: bfloat16 [4, 256, 2560], P(('group', 'cfg'), ('patch', 'head')), parts along dimension 0, may hold values from -12 to 12
- stale_key: bfloat16 [4, 256, 2560], P(('group', 'cfg'), 'patch', 'head'), parts along dimension 0, may hold values from -8 to 8
- stale_value: bfloat16 [4, 256, 2560], P(('group', 'cfg'), 'patch', 'head'), parts along dimension 0, may hold values from -12 to 12
- cross_query: bfloat16 [4, 256, 2560], P(('group', 'cfg'), ('patch', 'head')), parts along dimension 0, may hold values from -32 to 32
- text_key: bfloat16 [4, 512, 2560], P(('group', 'cfg'), None, 'head'), parts along dimension 0, may hold values from -8 to 8
- text_value: bfloat16 [4, 512, 2560], P(('group', 'cfg'), None, 'head'), parts along dimension 0, may hold values from -12 to 12
- text_mask: int32 [4, 512], P(('group', 'cfg')), parts along dimension 0, may hold values from 0 to 1, as said below
Outputs:
- self_mixed: bfloat16 [4, 256, 2560], P(('group', 'cfg'), ('patch', 'head')), parts along dimension 0
- cross_mixed: bfloat16 [4, 256, 2560], P(('group', 'cfg'), ('patch', 'head')), parts along dimension 0
There are 2 independent parts, one for each index of `group`. A program takes and returns all parts, laid end to end along the dimension named above; each array names one. Nothing has to cross between parts.
Inputs may be any that keep to these rules, and one draw needn't show every extreme that they name: In each branch the ones of text_mask form a prefix of 32 or more positions; in one of the two branches all 512 are ones, in the other some are zeros.
All inputs are finite; a program needn't handle non-finite values.
Results may differ from a plain program's by a relative error of at most 0.005.
Values may be sent and summed in bfloat16 or wider, within the bound.
No kernel may reach another device: no remote copies, remote signals or barrier semaphores. Data moves between devices by JAX's collectives and lax.ppermute only.
A program may use at most 128 MiB of HBM per device.

v0:
```python
import math

import jax
import jax.numpy as jnp
from jax import lax
from jax.experimental import pallas as pl
from jax.experimental.pallas import tpu as pltpu
from jax.sharding import PartitionSpec as P

HD = 128
SCALE = 1.0 / math.sqrt(HD)
TERMS = 3


def scores_of(queries, keys):
    return lax.dot_general(
        queries, keys, (((1,), (1,)), ((), ())), preferred_element_type=jnp.float32
    ) * SCALE


def weighted(weights, values):
    return lax.dot_general(
        weights, values, (((1,), (0,)), ((), ())), preferred_element_type=jnp.float32
    )


def softmax_parts(scores):
    tops = jnp.max(scores, axis=-1, keepdims=True)
    weights = jnp.exp(scores - tops)
    totals = jnp.sum(weights, axis=-1, keepdims=True)
    shape = (scores.shape[0], HD)
    shares = jnp.broadcast_to(1.0 / totals, shape)
    logs = jnp.broadcast_to(tops + jnp.log(totals), shape)
    return weights.astype(jnp.bfloat16), shares, logs


def lanes_of_logs(logs):
    lane = lax.broadcasted_iota(jnp.int32, logs[0].shape, 1)
    block = jnp.zeros(logs[0].shape, jnp.float32)
    for head, rest in enumerate(logs):
        for term in range(TERMS):
            part = rest.astype(jnp.bfloat16).astype(jnp.float32)
            block = jnp.where(lane == TERMS * head + term, part, block)
            rest = rest - part
    return block.astype(jnp.bfloat16)


def logs_of_lanes(block, head):
    lane = lax.broadcasted_iota(jnp.int32, (HD, HD), 0)
    picked = (lane >= TERMS * head) & (lane < TERMS * (head + 1))
    return weighted(block, jnp.where(picked, 1.0, 0.0).astype(block.dtype))


def run_all(copies, sems):
    started = []
    for index, (source, target) in enumerate(copies):
        started.append(pltpu.make_async_copy(source, target, sems.at[index]))
        started[-1].start()
    for copy in started:
        copy.wait()


def load_kernel(*refs):
    half = len(refs) // 2
    run_all(zip(refs[:half], refs[half:-1]), refs[-1])


def gate_kernel(*refs):
    pass


def head_lanes(head):
    return slice(head * HD, (head + 1) * HD)


def cross_kernel(shards, *refs):
    queries, (key_ref, value_ref, mask_ref) = refs[:shards], refs[shards : shards + 3]
    targets, (weights_ref, shares_ref) = refs[2 * shards + 2 : -2], refs[-2:]
    rows, cols = targets[0].shape
    usable = mask_ref[...] > 0
    for head in range(cols // HD):
        lanes = head_lanes(head)
        scores = scores_of(
            jnp.concatenate([ref[:, lanes] for ref in queries], axis=0), key_ref[0, :, lanes]
        )
        weights_ref[head], shares_ref[head], _ = softmax_parts(
            jnp.where(usable, scores, -jnp.inf)
        )
    for head in range(cols // HD):
        lanes = head_lanes(head)
        mixed = weighted(weights_ref[head], value_ref[0, :, lanes]) * shares_ref[head]
        for place, target in enumerate(targets):
            target[:, lanes] = mixed[place * rows : (place + 1) * rows].astype(target.dtype)


def solution(mesh):
    shards = mesh.shape["head"]
    patches = mesh.shape["patch"]
    axes = ("patch", "head")
    vmem = pl.BlockSpec(memory_space=pltpu.VMEM)
    hbm = pl.BlockSpec(memory_space=pltpu.HBM)
    anywhere = pl.BlockSpec(memory_space=pl.ANY)
    params = pltpu.CompilerParams(vmem_limit_bytes=32 * 1024 * 1024)

    def call(kernel, name, out_shape, operands, out_spec=vmem, in_spec=vmem, scratch=(), **more):
        return pl.pallas_call(
            kernel,
            out_shape=out_shape,
            in_specs=[in_spec] * len(operands),
            out_specs=jax.tree.map(lambda _: out_spec, out_shape),
            scratch_shapes=scratch,
            compiler_params=params,
            name=name,
            **more,
        )(*operands)

    def in_hbm(*arrays):
        return [pltpu.with_memory_space_constraint(a, pltpu.HBM) for a in arrays]

    def handed_on(arrays, others=(), **more):
        return call(
            gate_kernel,
            "gate",
            [jax.ShapeDtypeStruct(a.shape, a.dtype) for a in arrays],
            (*arrays, *others),
            anywhere,
            anywhere,
            input_output_aliases={i: i for i in range(len(arrays))},
            **more,
        )

    def per_device(
        fresh_query,
        fresh_key,
        fresh_value,
        stale_key,
        stale_value,
        cross_query,
        text_key,
        text_value,
        text_mask,
    ):
        rows, full = fresh_query.shape[1:]
        everyone = rows * shards
        patch_rows = stale_key.shape[1]
        text_rows = text_key.shape[1]
        kind = fresh_query.dtype
        cols = full // shards
        heads = cols // HD
        share = math.gcd(patches, heads)
        teams = patches // share
        width = cols // share
        share_heads = heads // share
        mates = [(j, s) for j in range(share) for s in range(shards) if (j, s) != (0, 0)]

        ring = list(range(0, teams, 2)) + list(range(1, teams, 2))[::-1]
        ring_next = dict(zip(ring, ring[1:] + ring[:1]))

        def moved(array, step, shift, turn):
            pairs = []
            for patch in range(patches):
                team, member = divmod(patch, share)
                team = ring_next[team] if step else team
                target = team * share + (member + shift) % share
                for shard in range(shards):
                    pairs.append(
                        (patch * shards + shard, target * shards + (shard + turn) % shards)
                    )
            return lax.ppermute(array, axes, pairs)

        def place_of(shift, turn, ref, size):
            shard = lax.rem(lax.axis_index("head") + turn, shards)
            member = lax.rem(lax.axis_index("patch") + shift, share)
            start = pl.multiple_of(shard * cols + member * width, HD)
            return ref.at[0, :, pl.ds(start, size)]

        over_patch = [mate for mate in mates if mate[0] != 0]
        near_blocks = [(turn, shift) for turn in range(shards) for shift in range(1, share)]
        near_width = len(near_blocks) * width
        stale_rows = 2 * patch_rows

        def fresh_start(shift, turn):
            return stale_rows if turn == 0 and shift != 0 else 0

        def message_rows(shift, turn):
            return fresh_start(shift, turn) + (3 if shift == 0 else 1) * rows

        def pack_kernel(query, key, value, old_key, old_value, cross, *refs):
            stale, own, refs = refs[:share], refs[share], refs[share + 1 :]
            crosses, messages = refs[:shards], refs[shards : shards + len(mates)]
            nears = refs[shards + len(mates) : -1]
            me = lax.rem(lax.axis_index("patch"), share)
            copies = []

            def stale_copies(shift, target):
                part = lax.rem(me + shift, share)
                lanes = pl.ds(pl.multiple_of(part * width, HD), width)
                for index, source in enumerate((old_key, old_value)):
                    block = pl.ds(index * patch_rows, patch_rows)
                    copies.append((source.at[0, :, lanes], target.at[block]))

            def fresh_copies(shift, turn, target, first):
                for index, source in enumerate((query, key, value)[: 3 if shift == 0 else 1]):
                    block = pl.ds(first + index * rows, rows)
                    copies.append((place_of(shift, turn, source, width), target.at[block]))

            for (shift, turn), message in zip(mates, messages):
                first = fresh_start(shift, turn)
                if first:
                    stale_copies(shift, message)
                fresh_copies(shift, turn, message, first)
            for shift in range(share):
                stale_copies(shift, stale[shift])
            fresh_copies(0, 0, own, 0)
            for turn, target in enumerate(crosses):
                shard = lax.rem(lax.axis_index("head") + turn, shards)
                lanes = pl.ds(pl.multiple_of(shard * cols, HD), cols)
                copies.append((cross.at[0, :, lanes], target))
            for turn, target in enumerate(nears):
                for index, source in enumerate((query, key, value)[0 if turn == 0 else 1 :]):
                    for place, (other, shift) in enumerate(near_blocks):
                        block = target.at[pl.ds(index * rows, rows), pl.ds(place * width, width)]
                        copies.append((place_of(shift, turn + other, source, width), block))
            run_all(copies, refs[-1])

        packed_shapes = (
            [(stale_rows, width)] * share
            + [(3 * rows, width)]
            + [(rows, cols)] * shards
            + [(message_rows(*mate), width) for mate in mates]
        )
        if near_blocks:
            packed_shapes += [(3 * rows, near_width)] + [(2 * rows, near_width)] * (shards - 1)
        copy_count = 2 * share + 3 + shards + sum(
            (3 if mate[0] == 0 else 1) + (2 if fresh_start(*mate) else 0) for mate in mates
        )
        copy_count += len(near_blocks) * (2 * shards + 1)
        packed = call(
            pack_kernel,
            "pack",
            [pltpu.VMEM(shape, kind) for shape in packed_shapes],
            in_hbm(fresh_query, fresh_key, fresh_value, stale_key, stale_value, cross_query),
            in_spec=hbm,
            scratch=[pltpu.SemaphoreType.DMA((copy_count,))],
        )
        stale, own, packed = packed[:share], packed[share], packed[share + 1 :]
        crosses, messages = packed[:shards], packed[shards : shards + len(mates)]
        nears = packed[shards + len(mates) :]
        text = [text_key, text_value, text_mask]
        text = call(
            load_kernel,
            "load",
            [pltpu.VMEM(a.shape, a.dtype) for a in text],
            in_hbm(*text),
            in_spec=hbm,
            scratch=[pltpu.SemaphoreType.DMA((len(text),))],
        )

        nears = [
            moved(handed_on([a], text[-1:])[0], 0, 0, turn) if turn else a
            for turn, a in enumerate(nears)
        ]
        arrived = [
            moved(message, 0, *mate) for mate, message in zip(mates, messages)
        ]
        crosses = [crosses[0]] + [moved(a, 0, 0, turn) for turn, a in enumerate(crosses) if turn]

        pieces = []
        if teams > 1:
            latest = [moved(stale[shift], 1, shift, 0) for shift in range(share)]
            pieces += latest
            for _ in range(teams - 2):
                latest = [moved(piece, 1, 0, 0) for piece in latest]
                pieces += latest

        cost = pl.CostEstimate(flops=500000000, bytes_accessed=1800000, transcendentals=0)
        pieces = handed_on(pieces, cost_estimate=cost) if pieces else pieces

        from_shards = [a for (shift, _), a in zip(mates, arrived) if shift == 0]
        cross_own, *cross_away = call(
            lambda *refs: cross_kernel(shards, *refs),
            "cross",
            [pltpu.VMEM((rows, cols), kind)] * shards,
            (*crosses, *text, *from_shards),
            scratch=[
                pltpu.VMEM((heads, shards * rows, text_rows), kind),
                pltpu.VMEM((heads, shards * rows, HD), jnp.float32),
            ],
        )
        cross_back = [moved(a, 0, 0, -turn - 1) for turn, a in enumerate(cross_away)]

        def place_kernel(spots, size, *refs):
            run_all(
                [
                    (ref, place_of(shift, turn, refs[-2], size))
                    for (shift, turn), ref in zip(spots, refs[:-2])
                ],
                refs[-1],
            )

        def cross_place_kernel(*refs):
            copies = []
            for turn, ref in enumerate(refs[:-2]):
                shard = lax.rem(lax.axis_index("head") + turn, shards)
                start = pl.multiple_of(shard * cols, HD)
                copies.append((ref, refs[-2].at[0, :, pl.ds(start, cols)]))
            run_all(copies, refs[-1])

        whole = jax.ShapeDtypeStruct((1, rows, full), kind)
        cross_mixed = call(
            cross_place_kernel,
            "place_cross",
            whole,
            (cross_own, *cross_back),
            hbm,
            scratch=[pltpu.SemaphoreType.DMA((shards,))],
        )

        def near_kernel(*refs):
            own_ref, others, (sums_ref, logs_ref, weights_ref, shares_ref) = refs[0], refs[1:-4], refs[-4:]
            for index in range(near_width // HD):
                lanes = head_lanes(index)
                keys = [own_ref[rows : 2 * rows, lanes]] + [ref[:rows, lanes] for ref in others]
                scores = scores_of(own_ref[:rows, lanes], jnp.concatenate(keys, axis=0))
                weights_ref[index], shares_ref[index], logs_ref[index] = softmax_parts(scores)
            for index in range(near_width // HD):
                lanes = head_lanes(index)
                values = [own_ref[2 * rows :, lanes]] + [ref[rows:, lanes] for ref in others]
                sums = weighted(weights_ref[index], jnp.concatenate(values, axis=0))
                sums_ref[:, lanes] = sums * shares_ref[index]

        near = []
        if near_blocks:
            near = call(
                near_kernel,
                "near",
                [
                    pltpu.VMEM((rows, near_width), jnp.float32),
                    pltpu.VMEM((near_width // HD, rows, HD), jnp.float32),
                ],
                nears,
                scratch=[
                    pltpu.VMEM((near_width // HD, rows, everyone), kind),
                    pltpu.VMEM((near_width // HD, rows, HD), jnp.float32),
                ],
            )

        spots = [(0, 0)] + mates
        tokens = [own, *arrived]
        first_row = dict(zip(spots, [0] + [fresh_start(*mate) for mate in mates]))

        def token_rows(refs, shift, index, lanes):
            found = []
            for spot, ref in zip(spots, refs):
                if spot[0] == shift:
                    start = first_row[spot] + index * rows
                    found.append(ref[start : start + rows, lanes])
            return found

        def stale_of(refs, shift, index, lanes):
            own_stale, *others = refs[len(spots) :]
            found = []
            if shift != 0:
                found.append(own_stale)
            found += [
                ref for (other, turn), ref in zip(spots, refs) if turn == 0 and other not in (0, shift)
            ]
            block = slice(index * patch_rows, (index + 1) * patch_rows)
            return [ref[block, lanes] for ref in found + others]

        def weights_kernel(*refs):
            count = len(spots) + 1 + len(pieces)
            sources, targets, logs_of = refs[:count], refs[count:], {}
            for head in range(share_heads):
                lanes = head_lanes(head)
                for shift in range(share):
                    queries = token_rows(sources, shift, 0, lanes)
                    keys = stale_of(sources, shift, 0, lanes)
                    if shift == 0:
                        keys = token_rows(sources, shift, 1, lanes) + keys
                    weights, shares, logs = softmax_parts(
                        scores_of(jnp.concatenate(queries, axis=0), jnp.concatenate(keys, axis=0))
                    )
                    for turn in range(shards):
                        spot = spots.index((shift, turn))
                        block = slice(turn * rows, (turn + 1) * rows)
                        targets[2 * spot][head] = weights[block]
                        targets[2 * spot + 1][head] = shares[block]
                        logs_of.setdefault(spot, []).append(logs[block])
            for place, mate in enumerate(over_patch):
                targets[2 * len(spots) + place][...] = lanes_of_logs(logs_of[spots.index(mate)])

        def mix_kernel(shift, weights_ref, shares_ref, *refs):
            sources, target = refs[:-1], refs[-1]
            for head in range(share_heads):
                lanes = head_lanes(head)
                values = stale_of(sources, shift, 1, lanes)
                if shift == 0:
                    values = token_rows(sources, shift, 2, lanes) + values
                mixed = weighted(weights_ref[head], jnp.concatenate(values, axis=0))
                target[:, lanes] = (mixed * shares_ref[head]).astype(target.dtype)

        def mate_mix_kernel(shift, weights_ref, shares_ref, logs_ref, *refs):
            mix_kernel(shift, weights_ref, shares_ref, *refs[:-1], refs[-1].at[:, pl.ds(0, width)])
            refs[-1][:, width:] = logs_ref[...]

        def merge_kernel(*refs):
            (sums_ref, logs_ref), refs = refs[:2], refs[2:]
            for (shift, turn), far, target in zip(over_patch, refs, refs[len(over_patch) :]):
                first = near_blocks.index((turn, shift)) * share_heads
                for head in range(share_heads):
                    lanes = head_lanes(head)
                    far_logs, near_logs = logs_of_lanes(far[:, width:], head), logs_ref[first + head]
                    tops = jnp.maximum(far_logs, near_logs)
                    far_part, near_part = jnp.exp(far_logs - tops), jnp.exp(near_logs - tops)
                    mixed = far[:, lanes].astype(jnp.float32) * far_part
                    mixed += sums_ref[:, head_lanes(first + head)] * near_part
                    target[:, lanes] = (mixed / (far_part + near_part)).astype(target.dtype)

        sources = (*tokens, stale[0], *pieces)
        part_shapes = []
        for shift, _ in spots:
            seen = patch_rows * (patches if shift == 0 else patches - 1)
            part_shapes += [
                pltpu.VMEM((share_heads, rows, seen), kind),
                pltpu.VMEM((share_heads, rows, HD), jnp.float32),
            ]
        parts = call(
            weights_kernel,
            "weights",
            part_shapes + [pltpu.VMEM((rows, HD), kind)] * len(over_patch),
            sources,
        )

        def mixed(spot):
            pair, shift = parts[2 * spot : 2 * spot + 2], spots[spot][0]
            if shift == 0:
                kernel, shape = mix_kernel, (rows, width)
            else:
                kernel, shape = mate_mix_kernel, (rows, width + HD)
                pair = (*pair, parts[2 * len(spots) + over_patch.index(spots[spot])])
            return call(
                lambda *refs: kernel(shift, *refs), "mix", pltpu.VMEM(shape, kind), (*pair, *sources)
            )

        back = [
            moved(mixed(index), 0, -shift, -turn)
            for index, (shift, turn) in enumerate(spots)
            if index > 0
        ]
        if over_patch:
            back[shards - 1 :] = call(
                merge_kernel,
                "merge",
                [pltpu.VMEM((rows, width), kind)] * len(over_patch),
                (*near, *back[shards - 1 :]),
            )
        self_mixed = call(
            lambda *refs: place_kernel(spots, width, *refs),
            "place_self",
            whole,
            (mixed(0), *back),
            hbm,
            scratch=[pltpu.SemaphoreType.DMA((len(spots),))],
        )
        return (self_mixed, cross_mixed)

    token = P(("group", "cfg"), ("patch", "head"), None)
    stale = P(("group", "cfg"), "patch", "head")
    text = P(("group", "cfg"), None, "head")
    return jax.shard_map(
        per_device,
        mesh=mesh,
        in_specs=(token, token, token, stale, stale, token, text, text, P(("group", "cfg"), None)),
        out_specs=(token, token),
        check_vma=False,
    )
```

profile of v0, /device:TPU:0, one launch (start us, length us, event | category | flops | bytes accessed | tf_op | source)
XLA Modules:
  0.0 30.6 jit_solution(14144345011319771437)
XLA Ops:
  0.6 1.6 %pack.1 = (bf16[128,640]{1,0:T(8,128)(2,1)S(1)}, bf16[128,640]{1,0:T(8,128)(2,1)S(1)}, bf16[96,640]{1,0:T(8,128)(2,1)S(1)}, bf16[32,1280]{1,0:T(8,128)(2,1)S(1)}...) custom-call(bf16[1,32,2560]{2,1,0:T(8,128)(2,1)} %query.1, ...), custom_call_target="tpu_custom_call" | custom-call | tf_op jit(solution)/shard_map/pack/pallas_call | solution.py:106
  2.2 5.1 %collective-permute-start.4 = (bf16[128,640]{1,0:T(8,128)(2,1)S(1)}, bf16[128,640]{1,0:T(8,128)(2,1)S(1)}, u32[]{:S(2)}, u32[]{:S(2)}) collective-permute-start(bf16[128,640]{1,0:T(8,128)(2,1)S(1)} %get-tuple-element.38), channel_id=1, source_target_pairs={{0,12},{2,14},{4,8},{6,10},{8,4},{10,6},{12,0},{14,2},{1,13},{3,15... | collective-permute-start | bytes 491528 | tf_op jit(solution)/shard_map/ppermute | solution.py:169
  7.3 0.0 collective-permute-start.3
  7.3 0.6 %collective-permute-start.1 = (bf16[160,640]{1,0:T(8,128)(2,1)S(1)}, bf16[160,640]{1,0:T(8,128)(2,1)S(1)}, u32[]{:S(2)}, u32[]{:S(2)}) collective-permute-start(bf16[160,640]{1,0:T(8,128)(2,1)S(1)} %get-tuple-element.35), channel_id=1, source_target_pairs={{0,4},{2,6},{4,0},{6,2},{8,12},{10,14},{12,8},{14,10},{1,5},{3,7},... | collective-permute-start | bytes 614408 | tf_op jit(solution)/shard_map/ppermute | solution.py:169
  7.9 1.6 %collective-permute-start.9 = (bf16[32,1280]{1,0:T(8,128)(2,1)S(1)}, bf16[32,1280]{1,0:T(8,128)(2,1)S(1)}, u32[]{:S(2)}, u32[]{:S(2)}) collective-permute-start(bf16[32,1280]{1,0:T(8,128)(2,1)S(1)} %get-tuple-element.59), channel_id=1, source_target_pairs={{0,2},{2,0},{4,6},{6,4},{8,10},{10,8},{12,14},{14,12},{1,3},{3,1},... | collective-permute-start | bytes 245768 | tf_op jit(solution)/shard_map/ppermute | solution.py:169
  9.6 0.4 %collective-permute-start = (bf16[96,640]{1,0:T(8,128)(2,1)S(1)}, bf16[96,640]{1,0:T(8,128)(2,1)S(1)}, u32[]{:S(2)}, u32[]{:S(2)}) collective-permute-start(bf16[96,640]{1,0:T(8,128)(2,1)S(1)} %get-tuple-element.34), channel_id=1, source_target_pairs={{0,2},{2,0},{4,6},{6,4},{8,10},{10,8},{12,14},{14,12},{1,3},{3,1},... | collective-permute-start | bytes 368648 | tf_op jit(solution)/shard_map/ppermute | solution.py:169
  10.0 1.7 %load.1 = (bf16[1,512,1280]{2,1,0:T(8,128)(2,1)S(1)}, bf16[1,512,1280]{2,1,0:T(8,128)(2,1)S(1)}, s32[1,512]{1,0:T(1,128)S(1)}) custom-call(bf16[1,512,1280]{2,1,0:T(8,128)(2,1)} %refs_0_.1, bf16[1,512,1280]{2,1,0:T(8,128)(2,1)} %refs_1_.1, s32[1,512]{1,0:T(1,128)} %refs_2_.1), custom_call_target="tpu_custom_call" | custom-call | tf_op jit(solution)/shard_map/load/pallas_call | solution.py:106
  11.7 1.5 %collective-permute-done.9.refs_1_ = bf16[32,1280]{1,0:T(8,128)(2,1)S(1)} collective-permute-done((bf16[32,1280]{1,0:T(8,128)(2,1)S(1)}, bf16[32,1280]{1,0:T(8,128)(2,1)S(1)}, u32[]{:S(2)}, u32[]{:S(2)}) %collective-permute-start.9) | collective-permute-done | bytes 81952 | tf_op jit(solution)/shard_map/ppermute | solution.py:169
  13.2 1.2 %collective-permute-start.6 = (bf16[64,1280]{1,0:T(8,128)(2,1)S(1)}, bf16[64,1280]{1,0:T(8,128)(2,1)S(1)}, u32[]{:S(2)}, u32[]{:S(2)}) collective-permute-start(bf16[64,1280]{1,0:T(8,128)(2,1)S(1)} %gate.3), channel_id=1, source_target_pairs={{0,2},{2,0},{4,6},{6,4},{8,10},{10,8},{12,14},{14,12},{1,3},{3,1},... | collective-permute-start | bytes 491528 | tf_op jit(solution)/shard_map/ppermute | solution.py:169
  14.4 1.2 %collective-permute-done.refs_1_.refs_3_.refs_4_.refs_5_ = bf16[96,640]{1,0:T(8,128)(2,1)S(1)} collective-permute-done((bf16[96,640]{1,0:T(8,128)(2,1)S(1)}, bf16[96,640]{1,0:T(8,128)(2,1)S(1)}, u32[]{:S(2)}, u32[]{:S(2)}) %collective-permute-start) | collective-permute-done | bytes 122912 | tf_op jit(solution)/shard_map/ppermute | solution.py:169
  15.6 1.9 %collective-permute-start.2 = (bf16[32,640]{1,0:T(8,128)(2,1)S(1)}, bf16[32,640]{1,0:T(8,128)(2,1)S(1)}, u32[]{:S(2)}, u32[]{:S(2)}) collective-permute-start(bf16[32,640]{1,0:T(8,128)(2,1)S(1)} %get-tuple-element.36), channel_id=1, source_target_pairs={{0,6},{2,4},{4,2},{6,0},{8,14},{10,12},{12,10},{14,8},{1,7},{3,5},... | collective-permute-start | bytes 122888 | tf_op jit(solution)/shard_map/ppermute | solution.py:169
  17.5 0.9 %cross.3 = (bf16[32,1280]{1,0:T(8,128)(2,1)S(1)}, bf16[32,1280]{1,0:T(8,128)(2,1)S(1)}) custom-call(bf16[32,1280]{1,0:T(8,128)(2,1)S(1)} %get-tuple-element.58.refs_0_, bf16[32,1280]{1,0:T(8,128)(2,1)S(1)} %collective-permute-done.9.refs_1_, bf16[1,512,1280]{2,1,0:T(8,128)(2,1)S(1)} %get-tuple-element.60.refs_2_, ...), custom_call_target="tpu_custom_call" | custom-call | tf_op jit(solution)/shard_map/cross/pallas_call | solution.py:106
  18.4 0.0 collective-permute-done.4.refs_1_
  18.4 1.2 %collective-permute-start.10 = (bf16[32,1280]{1,0:T(8,128)(2,1)S(1)}, bf16[32,1280]{1,0:T(8,128)(2,1)S(1)}, u32[]{:S(2)}, u32[]{:S(2)}) collective-permute-start(bf16[32,1280]{1,0:T(8,128)(2,1)S(1)} %get-tuple-element.63), channel_id=1, source_target_pairs={{0,2},{2,0},{4,6},{6,4},{8,10},{10,8},{12,14},{14,12},{1,3},{3,1},... | collective-permute-start | bytes 245768 | tf_op jit(solution)/shard_map/ppermute | solution.py:169
  19.6 1.7 %collective-permute-done.3.refs_0_ = bf16[128,640]{1,0:T(8,128)(2,1)S(1)} collective-permute-done((bf16[128,640]{1,0:T(8,128)(2,1)S(1)}, bf16[128,640]{1,0:T(8,128)(2,1)S(1)}, u32[]{:S(2)}, u32[]{:S(2)}) %collective-permute-start.3) | collective-permute-done | bytes 163872 | tf_op jit(solution)/shard_map/ppermute | solution.py:169
  21.3 1.4 %collective-permute-done.2.refs_3_.refs_5_.refs_6_ = bf16[32,640]{1,0:T(8,128)(2,1)S(1)} collective-permute-done((bf16[32,640]{1,0:T(8,128)(2,1)S(1)}, bf16[32,640]{1,0:T(8,128)(2,1)S(1)}, u32[]{:S(2)}, u32[]{:S(2)}) %collective-permute-start.2) | collective-permute-done | bytes 40992 | tf_op jit(solution)/shard_map/ppermute | solution.py:169
  22.7 0.0 collective-permute-done.1.refs_2_.refs_4_.refs_5_
  22.7 0.6 %weights.1 = (bf16[5,32,256]{2,1,0:T(8,128)(2,1)S(1)}, f32[5,32,128]{2,1,0:T(8,128)S(1)}, bf16[5,32,256]{2,1,0:T(8,128)(2,1)S(1)}, f32[5,32,128]{2,1,0:T(8,128)S...) custom-call(bf16[96,640]{1,0:T(8,128)(2,1)S(1)} %get-tuple-element.3, ...), custom_call_target="tpu_custom_call" | custom-call | tf_op jit(solution)/shard_map/weights/pallas_call | solution.py:106
  23.2 0.2 mix.7
  23.4 0.4 %collective-permute-start.8 = (bf16[32,768]{1,0:T(8,128)(2,1)S(1)}, bf16[32,768]{1,0:T(8,128)(2,1)S(1)}, u32[]{:S(2)}, u32[]{:S(2)}) collective-permute-start(bf16[32,768]{1,0:T(8,128)(2,1)S(1)} %mix.7), channel_id=1, source_target_pairs={{0,6},{2,4},{4,2},{6,0},{8,14},{10,12},{12,10},{14,8},{1,7},{3,5},... | collective-permute-start | bytes 147464 | tf_op jit(solution)/shard_map/ppermute | solution.py:169
  23.8 0.2 mix.6
  24.0 1.6 %collective-permute-start.7 = (bf16[32,768]{1,0:T(8,128)(2,1)S(1)}, bf16[32,768]{1,0:T(8,128)(2,1)S(1)}, u32[]{:S(2)}, u32[]{:S(2)}) collective-permute-start(bf16[32,768]{1,0:T(8,128)(2,1)S(1)} %mix.6), channel_id=1, source_target_pairs={{0,4},{2,6},{4,0},{6,2},{8,12},{10,14},{12,8},{14,10},{1,5},{3,7},... | collective-permute-start | bytes 147464 | tf_op jit(solution)/shard_map/ppermute | solution.py:169
  25.6 0.2 mix.5
  25.8 1.7 %collective-permute-start.5 = (bf16[32,640]{1,0:T(8,128)(2,1)S(1)}, bf16[32,640]{1,0:T(8,128)(2,1)S(1)}, u32[]{:S(2)}, u32[]{:S(2)}) collective-permute-start(bf16[32,640]{1,0:T(8,128)(2,1)S(1)} %mix.5), channel_id=1, source_target_pairs={{0,2},{2,0},{4,6},{6,4},{8,10},{10,8},{12,14},{14,12},{1,3},{3,1},... | collective-permute-start | bytes 122888 | tf_op jit(solution)/shard_map/ppermute | solution.py:169
  27.5 0.0 collective-permute-done.6.refs_1_
  27.5 0.4 %near.1 = (f32[32,1280]{1,0:T(8,128)S(1)}, f32[10,32,128]{2,1,0:T(8,128)S(1)}) custom-call(bf16[96,1280]{1,0:T(8,128)(2,1)S(1)} %get-tuple-element.45.refs_0_, bf16[64,1280]{1,0:T(8,128)(2,1)S(1)} %collective-permute-done.6.refs_1_), custom_call_target="tpu_custom_call" | custom-call | tf_op jit(solution)/shard_map/near/pallas_call | solution.py:106
  27.9 0.2 mix.4.refs_0_
  28.1 0.0 collective-permute-done.10.refs_1_
  28.1 0.7 %place_cross.1 = bf16[1,32,2560]{2,1,0:T(8,128)(2,1)} custom-call(bf16[32,1280]{1,0:T(8,128)(2,1)S(1)} %get-tuple-element.62.refs_0_, bf16[32,1280]{1,0:T(8,128)(2,1)S(1)} %collective-permute-done.10.refs_1_), custom_call_target="tpu_custom_call" | custom-call | tf_op jit(solution)/shard_map/place_cross/pallas_call | solution.py:106
  28.8 0.0 collective-permute-done.8.refs_3_
  28.8 0.0 collective-permute-done.7.refs_2_
  28.8 0.2 merge.1
  29.1 0.8 %collective-permute-done.5.refs_1_ = bf16[32,640]{1,0:T(8,128)(2,1)S(1)} collective-permute-done((bf16[32,640]{1,0:T(8,128)(2,1)S(1)}, bf16[32,640]{1,0:T(8,128)(2,1)S(1)}, u32[]{:S(2)}, u32[]{:S(2)}) %collective-permute-start.5) | collective-permute-done | bytes 40992 | tf_op jit(solution)/shard_map/ppermute | solution.py:169
  29.9 0.7 %place_self.1 = bf16[1,32,2560]{2,1,0:T(8,128)(2,1)} custom-call(bf16[32,640]{1,0:T(8,128)(2,1)S(1)} %mix.4.refs_0_, bf16[32,640]{1,0:T(8,128)(2,1)S(1)} %collective-permute-done.5.refs_1_, bf16[32,640]{1,0:T(8,128)(2,1)S(1)} %get-tuple-element.56.refs_2_, bf16[32,640]{1,0:T(8,128)(2,1)S(1)} %get-tuple-element.57.refs_3_), custom_call_target="tpu_custom_call" | custom-call | tf_op jit(solution)/shard_map/place_self/pallas_call | solution.py:106
  (2 shorter events, 0.0 us)
Async XLA Ops:
  2.2 16.2 %collective-permute-start.4 = (bf16[128,640]{1,0:T(8,128)(2,1)S(1)}, bf16[128,640]{1,0:T(8,128)(2,1)S(1)}, u32[]{:S(2)}, u32[]{:S(2)}) collective-permute-start(bf16[128,640]{1,0:T(8,128)(2,1)S(1)} %get-tuple-element.38), channel_id=1, source_target_pairs={{0,12},{2,14},{4,8},{6,10},{8,4},{10,6},{12,0},{14,2},{1,13},{3,15... | collective-permute-start | bytes 491528 | tf_op jit(solution)/shard_map/ppermute | solution.py:169
  7.3 14.0 %collective-permute-start.3 = (bf16[128,640]{1,0:T(8,128)(2,1)S(1)}, bf16[128,640]{1,0:T(8,128)(2,1)S(1)}, u32[]{:S(2)}, u32[]{:S(2)}) collective-permute-start(bf16[128,640]{1,0:T(8,128)(2,1)S(1)} %get-tuple-element.37.refs_4_.refs_6_.refs_7_), channel_id=1, source_target_pairs={{0,8},{2,10},{4,12},{6,14},{8,0},{10,2},{12,4},{14,6},{1,9},{3,11}... | collective-permute-start | bytes 491528 | tf_op jit(solution)/shard_map/ppermute | solution.py:169
  7.3 15.4 %collective-permute-start.1 = (bf16[160,640]{1,0:T(8,128)(2,1)S(1)}, bf16[160,640]{1,0:T(8,128)(2,1)S(1)}, u32[]{:S(2)}, u32[]{:S(2)}) collective-permute-start(bf16[160,640]{1,0:T(8,128)(2,1)S(1)} %get-tuple-element.35), channel_id=1, source_target_pairs={{0,4},{2,6},{4,0},{6,2},{8,12},{10,14},{12,8},{14,10},{1,5},{3,7},... | collective-permute-start | bytes 614408 | tf_op jit(solution)/shard_map/ppermute | solution.py:169
  7.9 5.2 %collective-permute-start.9 = (bf16[32,1280]{1,0:T(8,128)(2,1)S(1)}, bf16[32,1280]{1,0:T(8,128)(2,1)S(1)}, u32[]{:S(2)}, u32[]{:S(2)}) collective-permute-start(bf16[32,1280]{1,0:T(8,128)(2,1)S(1)} %get-tuple-element.59), channel_id=1, source_target_pairs={{0,2},{2,0},{4,6},{6,4},{8,10},{10,8},{12,14},{14,12},{1,3},{3,1},... | collective-permute-start | bytes 245768 | tf_op jit(solution)/shard_map/ppermute | solution.py:169
  9.6 6.0 %collective-permute-start = (bf16[96,640]{1,0:T(8,128)(2,1)S(1)}, bf16[96,640]{1,0:T(8,128)(2,1)S(1)}, u32[]{:S(2)}, u32[]{:S(2)}) collective-permute-start(bf16[96,640]{1,0:T(8,128)(2,1)S(1)} %get-tuple-element.34), channel_id=1, source_target_pairs={{0,2},{2,0},{4,6},{6,4},{8,10},{10,8},{12,14},{14,12},{1,3},{3,1},... | collective-permute-start | bytes 368648 | tf_op jit(solution)/shard_map/ppermute | solution.py:169
  13.2 14.3 %collective-permute-start.6 = (bf16[64,1280]{1,0:T(8,128)(2,1)S(1)}, bf16[64,1280]{1,0:T(8,128)(2,1)S(1)}, u32[]{:S(2)}, u32[]{:S(2)}) collective-permute-start(bf16[64,1280]{1,0:T(8,128)(2,1)S(1)} %gate.3), channel_id=1, source_target_pairs={{0,2},{2,0},{4,6},{6,4},{8,10},{10,8},{12,14},{14,12},{1,3},{3,1},... | collective-permute-start | bytes 491528 | tf_op jit(solution)/shard_map/ppermute | solution.py:169
  15.6 7.1 %collective-permute-start.2 = (bf16[32,640]{1,0:T(8,128)(2,1)S(1)}, bf16[32,640]{1,0:T(8,128)(2,1)S(1)}, u32[]{:S(2)}, u32[]{:S(2)}) collective-permute-start(bf16[32,640]{1,0:T(8,128)(2,1)S(1)} %get-tuple-element.36), channel_id=1, source_target_pairs={{0,6},{2,4},{4,2},{6,0},{8,14},{10,12},{12,10},{14,8},{1,7},{3,5},... | collective-permute-start | bytes 122888 | tf_op jit(solution)/shard_map/ppermute | solution.py:169
  18.4 9.7 %collective-permute-start.10 = (bf16[32,1280]{1,0:T(8,128)(2,1)S(1)}, bf16[32,1280]{1,0:T(8,128)(2,1)S(1)}, u32[]{:S(2)}, u32[]{:S(2)}) collective-permute-start(bf16[32,1280]{1,0:T(8,128)(2,1)S(1)} %get-tuple-element.63), channel_id=1, source_target_pairs={{0,2},{2,0},{4,6},{6,4},{8,10},{10,8},{12,14},{14,12},{1,3},{3,1},... | collective-permute-start | bytes 245768 | tf_op jit(solution)/shard_map/ppermute | solution.py:169
  23.4 5.4 %collective-permute-start.8 = (bf16[32,768]{1,0:T(8,128)(2,1)S(1)}, bf16[32,768]{1,0:T(8,128)(2,1)S(1)}, u32[]{:S(2)}, u32[]{:S(2)}) collective-permute-start(bf16[32,768]{1,0:T(8,128)(2,1)S(1)} %mix.7), channel_id=1, source_target_pairs={{0,6},{2,4},{4,2},{6,0},{8,14},{10,12},{12,10},{14,8},{1,7},{3,5},... | collective-permute-start | bytes 147464 | tf_op jit(solution)/shard_map/ppermute | solution.py:169
  24.0 4.8 %collective-permute-start.7 = (bf16[32,768]{1,0:T(8,128)(2,1)S(1)}, bf16[32,768]{1,0:T(8,128)(2,1)S(1)}, u32[]{:S(2)}, u32[]{:S(2)}) collective-permute-start(bf16[32,768]{1,0:T(8,128)(2,1)S(1)} %mix.6), channel_id=1, source_target_pairs={{0,4},{2,6},{4,0},{6,2},{8,12},{10,14},{12,8},{14,10},{1,5},{3,7},... | collective-permute-start | bytes 147464 | tf_op jit(solution)/shard_map/ppermute | solution.py:169
  25.8 4.1 %collective-permute-start.5 = (bf16[32,640]{1,0:T(8,128)(2,1)S(1)}, bf16[32,640]{1,0:T(8,128)(2,1)S(1)}, u32[]{:S(2)}, u32[]{:S(2)}) collective-permute-start(bf16[32,640]{1,0:T(8,128)(2,1)S(1)} %mix.5), channel_id=1, source_target_pairs={{0,2},{2,0},{4,6},{6,4},{8,10},{10,8},{12,14},{14,12},{1,3},{3,1},... | collective-permute-start | bytes 122888 | tf_op jit(solution)/shard_map/ppermute | solution.py:169
where the time goes:
time: 30.8 us; the launch traced here: 30.6 us
  starting transfers between devices  15.8 us (51%)
  Pallas kernels  7.51 us (24%)
  waiting for transfers between devices  6.56 us (21%)
  between operations  0.74 us (2%)
    ppermute x11, starting transfers between devices, moved(): return lax.ppermute(array, axes, pairs)  15.8 us
    pallas_call x14, Pallas kernels, call(): pl.pallas_call(kernel, out_shape=out_shape, in_specs=[in_spec] * len(oper...  7.51 us
    ppermute x11, waiting for transfers between devices, moved(): return lax.ppermute(array, axes, pairs)  6.56 us
  transfers between devices with their start and end apart: 11, of which 5 were waited for; matrix products, arithmetic and copies ran while one was open for 0% of the time, Pallas kernels for 17%

commit v1 on v0

--- a/solution.py
+++ b/solution.py
@@ -73,10 +73,10 @@
     return slice(head * HD, (head + 1) * HD)
 
 
-def cross_kernel(shards, *refs):
+def cross_kernel(shards, nears, *refs):
     queries, (key_ref, value_ref, mask_ref) = refs[:shards], refs[shards : shards + 3]
-    targets, (weights_ref, shares_ref) = refs[2 * shards + 2 : -2], refs[-2:]
-    rows, cols = targets[0].shape
+    own, away, (weights_ref, shares_ref) = refs[-2 - shards], refs[-1 - shards : -2], refs[-2:]
+    rows, cols = own.shape
     usable = mask_ref[...] > 0
     for head in range(cols // HD):
         lanes = head_lanes(head)
@@ -86,11 +86,17 @@
         weights_ref[head], shares_ref[head], _ = softmax_parts(
             jnp.where(usable, scores, -jnp.inf)
         )
+    for source, target in zip(refs[shards + 3 : shards + 3 + nears], away):
+        target[target.shape[0] - source.shape[0] :, :] = source[...]
     for head in range(cols // HD):
         lanes = head_lanes(head)
         mixed = weighted(weights_ref[head], value_ref[0, :, lanes]) * shares_ref[head]
-        for place, target in enumerate(targets):
-            target[:, lanes] = mixed[place * rows : (place + 1) * rows].astype(target.dtype)
+        own[:, lanes] = mixed[:rows].astype(own.dtype)
+        for turn, target in enumerate(away, 1):
+            part, inner = divmod(head * HD, target.shape[1])
+            block = slice(part * rows, (part + 1) * rows)
+            mine = mixed[turn * rows : (turn + 1) * rows].astype(target.dtype)
+            target[block, inner : inner + HD] = mine
 
 
 def solution(mesh):
@@ -117,12 +123,12 @@
     def in_hbm(*arrays):
         return [pltpu.with_memory_space_constraint(a, pltpu.HBM) for a in arrays]
 
-    def handed_on(arrays, others=(), **more):
+    def handed_on(arrays, **more):
         return call(
             gate_kernel,
             "gate",
             [jax.ShapeDtypeStruct(a.shape, a.dtype) for a in arrays],
-            (*arrays, *others),
+            arrays,
             anywhere,
             anywhere,
             input_output_aliases={i: i for i in range(len(arrays))},
@@ -177,6 +183,7 @@
         over_patch = [mate for mate in mates if mate[0] != 0]
         near_blocks = [(turn, shift) for turn in range(shards) for shift in range(1, share)]
         near_width = len(near_blocks) * width
+        back_rows = (share + 2 * len(near_blocks)) * rows
         stale_rows = 2 * patch_rows
 
         def fresh_start(shift, turn):
@@ -217,10 +224,16 @@
                 lanes = pl.ds(pl.multiple_of(shard * cols, HD), cols)
                 copies.append((cross.at[0, :, lanes], target))
             for turn, target in enumerate(nears):
-                for index, source in enumerate((query, key, value)[0 if turn == 0 else 1 :]):
-                    for place, (other, shift) in enumerate(near_blocks):
-                        block = target.at[pl.ds(index * rows, rows), pl.ds(place * width, width)]
-                        copies.append((place_of(shift, turn + other, source, width), block))
+                for place, (other, shift) in enumerate(near_blocks):
+                    for index, source in enumerate((query, key, value)):
+                        if turn == 0:
+                            block = pl.ds((3 * place + index) * rows, rows)
+                        elif index > 0:
+                            block = pl.ds((2 * place + index - 1) * rows, rows)
+                        else:
+                            continue
+                        spot = place_of(shift, other + shards - turn, source, width)
+                        copies.append((spot, target.at[block]))
             run_all(copies, refs[-1])
 
         packed_shapes = (
@@ -230,7 +243,8 @@
             + [(message_rows(*mate), width) for mate in mates]
         )
         if near_blocks:
-            packed_shapes += [(3 * rows, near_width)] + [(2 * rows, near_width)] * (shards - 1)
+            near_rows = [3 * rows * len(near_blocks)] + [2 * rows * len(near_blocks)] * (shards - 1)
+            packed_shapes += [(height, width) for height in near_rows]
         copy_count = 2 * share + 3 + shards + sum(
             (3 if mate[0] == 0 else 1) + (2 if fresh_start(*mate) else 0) for mate in mates
         )
@@ -256,10 +270,7 @@
             scratch=[pltpu.SemaphoreType.DMA((len(text),))],
         )
 
-        nears = [
-            moved(handed_on([a], text[-1:])[0], 0, 0, turn) if turn else a
-            for turn, a in enumerate(nears)
-        ]
+
         arrived = [
             moved(message, 0, *mate) for mate, message in zip(mates, messages)
         ]
@@ -273,15 +284,19 @@
                 latest = [moved(piece, 1, 0, 0) for piece in latest]
                 pieces += latest
 
-        cost = pl.CostEstimate(flops=500000000, bytes_accessed=1800000, transcendentals=0)
-        pieces = handed_on(pieces, cost_estimate=cost) if pieces else pieces
+        if teams * share > 1:
+            first = len(mates) - len(over_patch)
+            cost = pl.CostEstimate(flops=3000000000, bytes_accessed=10800000, transcendentals=0)
+            found = list(handed_on([*arrived[first:], *pieces], cost_estimate=cost))
+            arrived[first:], pieces = found[: len(over_patch)], found[len(over_patch) :]
 
         from_shards = [a for (shift, _), a in zip(mates, arrived) if shift == 0]
         cross_own, *cross_away = call(
-            lambda *refs: cross_kernel(shards, *refs),
+            lambda *refs: cross_kernel(shards, len(nears[1:]), *refs),
             "cross",
-            [pltpu.VMEM((rows, cols), kind)] * shards,
-            (*crosses, *text, *from_shards),
+            [pltpu.VMEM((rows, cols), kind)]
+            + [pltpu.VMEM((back_rows, width), kind)] * (shards - 1),
+            (*crosses, *text, *nears[1:], *from_shards),
             scratch=[
                 pltpu.VMEM((heads, shards * rows, text_rows), kind),
                 pltpu.VMEM((heads, shards * rows, HD), jnp.float32),
@@ -302,8 +317,14 @@
             copies = []
             for turn, ref in enumerate(refs[:-2]):
                 shard = lax.rem(lax.axis_index("head") + turn, shards)
-                start = pl.multiple_of(shard * cols, HD)
-                copies.append((ref, refs[-2].at[0, :, pl.ds(start, cols)]))
+                if turn == 0:
+                    start = pl.multiple_of(shard * cols, HD)
+                    copies.append((ref, refs[-2].at[0, :, pl.ds(start, cols)]))
+                    continue
+                for part in range(share):
+                    start = pl.multiple_of(shard * cols + part * width, HD)
+                    block = ref.at[pl.ds(part * rows, rows)]
+                    copies.append((block, refs[-2].at[0, :, pl.ds(start, width)]))
             run_all(copies, refs[-1])
 
         whole = jax.ShapeDtypeStruct((1, rows, full), kind)
@@ -313,21 +334,28 @@
             whole,
             (cross_own, *cross_back),
             hbm,
-            scratch=[pltpu.SemaphoreType.DMA((shards,))],
+            scratch=[pltpu.SemaphoreType.DMA((1 + (shards - 1) * share,))],
         )
 
         def near_kernel(*refs):
             own_ref, others, (sums_ref, logs_ref, weights_ref, shares_ref) = refs[0], refs[1:-4], refs[-4:]
-            for index in range(near_width // HD):
-                lanes = head_lanes(index)
-                keys = [own_ref[rows : 2 * rows, lanes]] + [ref[:rows, lanes] for ref in others]
-                scores = scores_of(own_ref[:rows, lanes], jnp.concatenate(keys, axis=0))
-                weights_ref[index], shares_ref[index], logs_ref[index] = softmax_parts(scores)
-            for index in range(near_width // HD):
-                lanes = head_lanes(index)
-                values = [own_ref[2 * rows :, lanes]] + [ref[rows:, lanes] for ref in others]
-                sums = weighted(weights_ref[index], jnp.concatenate(values, axis=0))
-                sums_ref[:, lanes] = sums * shares_ref[index]
+
+            def rows_of(index, head):
+                place, head = divmod(head, share_heads)
+                lanes = head_lanes(head)
+                start = (3 * place + index) * rows
+                found = [own_ref[start : start + rows, lanes]]
+                start = (share + 2 * place + index - 1) * rows
+                for ref in others if index > 0 else ():
+                    found.append(ref[start : start + rows, lanes])
+                return jnp.concatenate(found, axis=0)
+
+            for head in range(near_width // HD):
+                scores = scores_of(rows_of(0, head), rows_of(1, head))
+                weights_ref[head], shares_ref[head], logs_ref[head] = softmax_parts(scores)
+            for head in range(near_width // HD):
+                sums = weighted(weights_ref[head], rows_of(2, head))
+                sums_ref[:, head_lanes(head)] = sums * shares_ref[head]
 
         near = []
         if near_blocks:
@@ -338,7 +366,7 @@
                     pltpu.VMEM((rows, near_width), jnp.float32),
                     pltpu.VMEM((near_width // HD, rows, HD), jnp.float32),
                 ],
-                nears,
+                (nears[0], *cross_back),
                 scratch=[
                     pltpu.VMEM((near_width // HD, rows, everyone), kind),
                     pltpu.VMEM((near_width // HD, rows, HD), jnp.float32),

time: 30.8 us -> 31.5 us (1.023)
  waiting for transfers between devices: 6.56 us -> 8.63 us
  starting transfers between devices: 15.8 us -> 14.4 us
    ppermute x11 -> x10, waiting for transfers between devices: 6.56 us -> 8.63 us  [moved(): return lax.ppermute(array, axes, pairs)]
    ppermute x11 -> x10, starting transfers between devices: 15.8 us -> 14.4 us  [moved(): return lax.ppermute(array, axes, pairs)]
    pallas_call x14 -> x13, Pallas kernels: 7.51 us -> 7.51 us  [call(): pl.pallas_call(kernel, out_shape=out_shape, in_specs=[in_spec] * len(oper...]
  transfers between devices with their start and end apart: 11 -> 10, of which waited for: 5 -> 4; matrix products, arithmetic and copies ran while one was open for 0% -> 0% of each run, Pallas kernels for 17% -> 17%
where the time goes in v1:
time: 31.5 us; the launch traced here: 31.3 us
  starting transfers between devices  14.4 us (46%)
  waiting for transfers between devices  8.63 us (27%)
  Pallas kernels  7.51 us (24%)
  between operations  0.72 us (2%)
    ppermute x10, starting transfers between devices, moved(): return lax.ppermute(array, axes, pairs)  14.4 us
    ppermute x10, waiting for transfers between devices, moved(): return lax.ppermute(array, axes, pairs)  8.63 us
    pallas_call x13, Pallas kernels, call(): pl.pallas_call(kernel, out_shape=out_shape, in_specs=[in_spec] * len(oper...  7.51 us
  transfers between devices with their start and end apart: 10, of which 4 were waited for; matrix products, arithmetic and copies ran while one was open for 0% of the time, Pallas kernels for 17%

profile of v1, /device:TPU:0, one launch (start us, length us, event | category | flops | bytes accessed | tf_op | source)
XLA Modules:
  0.0 31.3 jit_solution(2517526975275278653)
XLA Ops:
  0.6 1.6 %pack.1 = (bf16[128,640]{1,0:T(8,128)(2,1)S(1)}, bf16[128,640]{1,0:T(8,128)(2,1)S(1)}, bf16[96,640]{1,0:T(8,128)(2,1)S(1)}, bf16[32,1280]{1,0:T(8,128)(2,1)S(1)}...) custom-call(bf16[1,32,2560]{2,1,0:T(8,128)(2,1)} %query.1, ...), custom_call_target="tpu_custom_call" | custom-call | tf_op jit(solution)/shard_map/pack/pallas_call | solution.py:112
  2.2 3.1 %collective-permute-start.1 = (bf16[160,640]{1,0:T(8,128)(2,1)S(1)}, bf16[160,640]{1,0:T(8,128)(2,1)S(1)}, u32[]{:S(2)}, u32[]{:S(2)}) collective-permute-start(bf16[160,640]{1,0:T(8,128)(2,1)S(1)} %get-tuple-element.37), channel_id=1, source_target_pairs={{0,4},{2,6},{4,0},{6,2},{8,12},{10,14},{12,8},{14,10},{1,5},{3,7},... | collective-permute-start | bytes 614408 | tf_op jit(solution)/shard_map/ppermute | solution.py:175
  5.3 2.5 %collective-permute-start.4 = (bf16[128,640]{1,0:T(8,128)(2,1)S(1)}, bf16[128,640]{1,0:T(8,128)(2,1)S(1)}, u32[]{:S(2)}, u32[]{:S(2)}) collective-permute-start(bf16[128,640]{1,0:T(8,128)(2,1)S(1)} %get-tuple-element.40), channel_id=1, source_target_pairs={{0,12},{2,14},{4,8},{6,10},{8,4},{10,6},{12,0},{14,2},{1,13},{3,15... | collective-permute-start | bytes 491528 | tf_op jit(solution)/shard_map/ppermute | solution.py:175
  7.8 0.1 collective-permute-start.3
  7.9 1.5 %collective-permute-start = (bf16[96,640]{1,0:T(8,128)(2,1)S(1)}, bf16[96,640]{1,0:T(8,128)(2,1)S(1)}, u32[]{:S(2)}, u32[]{:S(2)}) collective-permute-start(bf16[96,640]{1,0:T(8,128)(2,1)S(1)} %get-tuple-element.36), channel_id=1, source_target_pairs={{0,2},{2,0},{4,6},{6,4},{8,10},{10,8},{12,14},{14,12},{1,3},{3,1},... | collective-permute-start | bytes 368648 | tf_op jit(solution)/shard_map/ppermute | solution.py:175
  9.4 0.5 %collective-permute-start.6 = (bf16[32,1280]{1,0:T(8,128)(2,1)S(1)}, bf16[32,1280]{1,0:T(8,128)(2,1)S(1)}, u32[]{:S(2)}, u32[]{:S(2)}) collective-permute-start(bf16[32,1280]{1,0:T(8,128)(2,1)S(1)} %get-tuple-element.51), channel_id=1, source_target_pairs={{0,2},{2,0},{4,6},{6,4},{8,10},{10,8},{12,14},{14,12},{1,3},{3,1},... | collective-permute-start | bytes 245768 | tf_op jit(solution)/shard_map/ppermute | solution.py:175
  9.9 4.2 %collective-permute-done.6.refs_1_ = bf16[32,1280]{1,0:T(8,128)(2,1)S(1)} collective-permute-done((bf16[32,1280]{1,0:T(8,128)(2,1)S(1)}, bf16[32,1280]{1,0:T(8,128)(2,1)S(1)}, u32[]{:S(2)}, u32[]{:S(2)}) %collective-permute-start.6) | collective-permute-done | bytes 81952 | tf_op jit(solution)/shard_map/ppermute | solution.py:175
  14.1 2.4 %collective-permute-start.2 = (bf16[32,640]{1,0:T(8,128)(2,1)S(1)}, bf16[32,640]{1,0:T(8,128)(2,1)S(1)}, u32[]{:S(2)}, u32[]{:S(2)}) collective-permute-start(bf16[32,640]{1,0:T(8,128)(2,1)S(1)} %get-tuple-element.38), channel_id=1, source_target_pairs={{0,6},{2,4},{4,2},{6,0},{8,14},{10,12},{12,10},{14,8},{1,7},{3,5},... | collective-permute-start | bytes 122888 | tf_op jit(solution)/shard_map/ppermute | solution.py:175
  16.6 1.7 %load.1 = (bf16[1,512,1280]{2,1,0:T(8,128)(2,1)S(1)}, bf16[1,512,1280]{2,1,0:T(8,128)(2,1)S(1)}, s32[1,512]{1,0:T(1,128)S(1)}) custom-call(bf16[1,512,1280]{2,1,0:T(8,128)(2,1)} %refs_0_.1, bf16[1,512,1280]{2,1,0:T(8,128)(2,1)} %refs_1_.1, s32[1,512]{1,0:T(1,128)} %refs_2_.1), custom_call_target="tpu_custom_call" | custom-call | tf_op jit(solution)/shard_map/load/pallas_call | solution.py:112
  18.3 0.0 collective-permute-done.refs_1_.refs_3_.refs_6_.refs_4_
  18.3 0.9 %cross.3 = (bf16[32,1280]{1,0:T(8,128)(2,1)S(1)}, bf16[192,640]{1,0:T(8,128)(2,1)S(1)}) custom-call(bf16[32,1280]{1,0:T(8,128)(2,1)S(1)} %get-tuple-element.50.refs_0_, bf16[32,1280]{1,0:T(8,128)(2,1)S(1)} %collective-permute-done.6.refs_1_, bf16[1,512,1280]{2,1,0:T(8,128)(2,1)S(1)} %get-tuple-element.52.refs_2_, ...), custom_call_target="tpu_custom_call" | custom-call | tf_op jit(solution)/shard_map/cross/pallas_call | solution.py:112
  19.2 0.6 %collective-permute-start.7 = (bf16[192,640]{1,0:T(8,128)(2,1)S(1)}, bf16[192,640]{1,0:T(8,128)(2,1)S(1)}, u32[]{:S(2)}, u32[]{:S(2)}) collective-permute-start(bf16[192,640]{1,0:T(8,128)(2,1)S(1)} %get-tuple-element.56), channel_id=1, source_target_pairs={{0,2},{2,0},{4,6},{6,4},{8,10},{10,8},{12,14},{14,12},{1,3},{3,1},... | collective-permute-start | bytes 737288 | tf_op jit(solution)/shard_map/ppermute | solution.py:175
  19.8 0.0 collective-permute-done.2.refs_1_
  19.8 0.0 collective-permute-done.4.refs_3_
  19.8 2.5 %collective-permute-done.3.refs_2_ = bf16[128,640]{1,0:T(8,128)(2,1)S(1)} collective-permute-done((bf16[128,640]{1,0:T(8,128)(2,1)S(1)}, bf16[128,640]{1,0:T(8,128)(2,1)S(1)}, u32[]{:S(2)}, u32[]{:S(2)}) %collective-permute-start.3) | collective-permute-done | bytes 163872 | tf_op jit(solution)/shard_map/ppermute | solution.py:175
  22.3 0.0 collective-permute-done.1.refs_0_
  22.3 0.6 %weights.1 = (bf16[5,32,256]{2,1,0:T(8,128)(2,1)S(1)}, f32[5,32,128]{2,1,0:T(8,128)S(1)}, bf16[5,32,256]{2,1,0:T(8,128)(2,1)S(1)}, f32[5,32,128]{2,1,0:T(8,128)S...) custom-call(bf16[96,640]{1,0:T(8,128)(2,1)S(1)} %get-tuple-element.3, ...), custom_call_target="tpu_custom_call" | custom-call | tf_op jit(solution)/shard_map/weights/pallas_call | solution.py:112
  22.9 0.2 mix.7
  23.1 0.8 %collective-permute-start.9 = (bf16[32,768]{1,0:T(8,128)(2,1)S(1)}, bf16[32,768]{1,0:T(8,128)(2,1)S(1)}, u32[]{:S(2)}, u32[]{:S(2)}) collective-permute-start(bf16[32,768]{1,0:T(8,128)(2,1)S(1)} %mix.7), channel_id=1, source_target_pairs={{0,6},{2,4},{4,2},{6,0},{8,14},{10,12},{12,10},{14,8},{1,7},{3,5},... | collective-permute-start | bytes 147464 | tf_op jit(solution)/shard_map/ppermute | solution.py:175
  23.9 0.2 mix.6
  24.1 2.3 %collective-permute-start.8 = (bf16[32,768]{1,0:T(8,128)(2,1)S(1)}, bf16[32,768]{1,0:T(8,128)(2,1)S(1)}, u32[]{:S(2)}, u32[]{:S(2)}) collective-permute-start(bf16[32,768]{1,0:T(8,128)(2,1)S(1)} %mix.6), channel_id=1, source_target_pairs={{0,4},{2,6},{4,0},{6,2},{8,12},{10,14},{12,8},{14,10},{1,5},{3,7},... | collective-permute-start | bytes 147464 | tf_op jit(solution)/shard_map/ppermute | solution.py:175
  26.4 0.2 mix.5
  26.5 0.6 %collective-permute-start.5 = (bf16[32,640]{1,0:T(8,128)(2,1)S(1)}, bf16[32,640]{1,0:T(8,128)(2,1)S(1)}, u32[]{:S(2)}, u32[]{:S(2)}) collective-permute-start(bf16[32,640]{1,0:T(8,128)(2,1)S(1)} %mix.5), channel_id=1, source_target_pairs={{0,2},{2,0},{4,6},{6,4},{8,10},{10,8},{12,14},{14,12},{1,3},{3,1},... | collective-permute-start | bytes 122888 | tf_op jit(solution)/shard_map/ppermute | solution.py:175
  27.1 0.2 mix.4.refs_0_
  27.3 0.0 collective-permute-done.7.refs_1_
  27.3 0.7 %place_cross.1 = bf16[1,32,2560]{2,1,0:T(8,128)(2,1)} custom-call(bf16[32,1280]{1,0:T(8,128)(2,1)S(1)} %get-tuple-element.67.refs_0_, bf16[192,640]{1,0:T(8,128)(2,1)S(1)} %collective-permute-done.7.refs_1_), custom_call_target="tpu_custom_call" | custom-call | tf_op jit(solution)/shard_map/place_cross/pallas_call | solution.py:112
  28.0 0.4 %near.1 = (f32[32,1280]{1,0:T(8,128)S(1)}, f32[10,32,128]{2,1,0:T(8,128)S(1)}) custom-call(bf16[192,640]{1,0:T(8,128)(2,1)S(1)} %get-tuple-element.49.refs_0_, bf16[192,640]{1,0:T(8,128)(2,1)S(1)} %collective-permute-done.7.refs_1_), custom_call_target="tpu_custom_call" | custom-call | tf_op jit(solution)/shard_map/near/pallas_call | solution.py:112
  28.5 0.0 collective-permute-done.9.refs_3_
  28.5 0.2 collective-permute-done.8.refs_2_
  28.7 0.2 merge.1
  28.9 1.7 %collective-permute-done.5.refs_1_ = bf16[32,640]{1,0:T(8,128)(2,1)S(1)} collective-permute-done((bf16[32,640]{1,0:T(8,128)(2,1)S(1)}, bf16[32,640]{1,0:T(8,128)(2,1)S(1)}, u32[]{:S(2)}, u32[]{:S(2)}) %collective-permute-start.5) | collective-permute-done | bytes 40992 | tf_op jit(solution)/shard_map/ppermute | solution.py:175
  30.6 0.7 %place_self.1 = bf16[1,32,2560]{2,1,0:T(8,128)(2,1)} custom-call(bf16[32,640]{1,0:T(8,128)(2,1)S(1)} %mix.4.refs_0_, bf16[32,640]{1,0:T(8,128)(2,1)S(1)} %collective-permute-done.5.refs_1_, bf16[32,640]{1,0:T(8,128)(2,1)S(1)} %get-tuple-element.65.refs_2_, bf16[32,640]{1,0:T(8,128)(2,1)S(1)} %get-tuple-element.66.refs_3_), custom_call_target="tpu_custom_call" | custom-call | tf_op jit(solution)/shard_map/place_self/pallas_call | solution.py:112
  (1 shorter events, 0.0 us)
Async XLA Ops:
  2.2 20.1 %collective-permute-start.1 = (bf16[160,640]{1,0:T(8,128)(2,1)S(1)}, bf16[160,640]{1,0:T(8,128)(2,1)S(1)}, u32[]{:S(2)}, u32[]{:S(2)}) collective-permute-start(bf16[160,640]{1,0:T(8,128)(2,1)S(1)} %get-tuple-element.37), channel_id=1, source_target_pairs={{0,4},{2,6},{4,0},{6,2},{8,12},{10,14},{12,8},{14,10},{1,5},{3,7},... | collective-permute-start | bytes 614408 | tf_op jit(solution)/shard_map/ppermute | solution.py:175
  5.3 14.6 %collective-permute-start.4 = (bf16[128,640]{1,0:T(8,128)(2,1)S(1)}, bf16[128,640]{1,0:T(8,128)(2,1)S(1)}, u32[]{:S(2)}, u32[]{:S(2)}) collective-permute-start(bf16[128,640]{1,0:T(8,128)(2,1)S(1)} %get-tuple-element.40), channel_id=1, source_target_pairs={{0,12},{2,14},{4,8},{6,10},{8,4},{10,6},{12,0},{14,2},{1,13},{3,15... | collective-permute-start | bytes 491528 | tf_op jit(solution)/shard_map/ppermute | solution.py:175
  7.8 14.6 %collective-permute-start.3 = (bf16[128,640]{1,0:T(8,128)(2,1)S(1)}, bf16[128,640]{1,0:T(8,128)(2,1)S(1)}, u32[]{:S(2)}, u32[]{:S(2)}) collective-permute-start(bf16[128,640]{1,0:T(8,128)(2,1)S(1)} %get-tuple-element.39.refs_4_.refs_6_.refs_7_), channel_id=1, source_target_pairs={{0,8},{2,10},{4,12},{6,14},{8,0},{10,2},{12,4},{14,6},{1,9},{3,11}... | collective-permute-start | bytes 491528 | tf_op jit(solution)/shard_map/ppermute | solution.py:175
  7.9 10.4 %collective-permute-start = (bf16[96,640]{1,0:T(8,128)(2,1)S(1)}, bf16[96,640]{1,0:T(8,128)(2,1)S(1)}, u32[]{:S(2)}, u32[]{:S(2)}) collective-permute-start(bf16[96,640]{1,0:T(8,128)(2,1)S(1)} %get-tuple-element.36), channel_id=1, source_target_pairs={{0,2},{2,0},{4,6},{6,4},{8,10},{10,8},{12,14},{14,12},{1,3},{3,1},... | collective-permute-start | bytes 368648 | tf_op jit(solution)/shard_map/ppermute | solution.py:175
  9.4 4.8 %collective-permute-start.6 = (bf16[32,1280]{1,0:T(8,128)(2,1)S(1)}, bf16[32,1280]{1,0:T(8,128)(2,1)S(1)}, u32[]{:S(2)}, u32[]{:S(2)}) collective-permute-start(bf16[32,1280]{1,0:T(8,128)(2,1)S(1)} %get-tuple-element.51), channel_id=1, source_target_pairs={{0,2},{2,0},{4,6},{6,4},{8,10},{10,8},{12,14},{14,12},{1,3},{3,1},... | collective-permute-start | bytes 245768 | tf_op jit(solution)/shard_map/ppermute | solution.py:175
  14.1 5.7 %collective-permute-start.2 = (bf16[32,640]{1,0:T(8,128)(2,1)S(1)}, bf16[32,640]{1,0:T(8,128)(2,1)S(1)}, u32[]{:S(2)}, u32[]{:S(2)}) collective-permute-start(bf16[32,640]{1,0:T(8,128)(2,1)S(1)} %get-tuple-element.38), channel_id=1, source_target_pairs={{0,6},{2,4},{4,2},{6,0},{8,14},{10,12},{12,10},{14,8},{1,7},{3,5},... | collective-permute-start | bytes 122888 | tf_op jit(solution)/shard_map/ppermute | solution.py:175
  19.2 8.1 %collective-permute-start.7 = (bf16[192,640]{1,0:T(8,128)(2,1)S(1)}, bf16[192,640]{1,0:T(8,128)(2,1)S(1)}, u32[]{:S(2)}, u32[]{:S(2)}) collective-permute-start(bf16[192,640]{1,0:T(8,128)(2,1)S(1)} %get-tuple-element.56), channel_id=1, source_target_pairs={{0,2},{2,0},{4,6},{6,4},{8,10},{10,8},{12,14},{14,12},{1,3},{3,1},... | collective-permute-start | bytes 737288 | tf_op jit(solution)/shard_map/ppermute | solution.py:175
  23.1 5.4 %collective-permute-start.9 = (bf16[32,768]{1,0:T(8,128)(2,1)S(1)}, bf16[32,768]{1,0:T(8,128)(2,1)S(1)}, u32[]{:S(2)}, u32[]{:S(2)}) collective-permute-start(bf16[32,768]{1,0:T(8,128)(2,1)S(1)} %mix.7), channel_id=1, source_target_pairs={{0,6},{2,4},{4,2},{6,0},{8,14},{10,12},{12,10},{14,8},{1,7},{3,5},... | collective-permute-start | bytes 147464 | tf_op jit(solution)/shard_map/ppermute | solution.py:175
  24.1 4.6 %collective-permute-start.8 = (bf16[32,768]{1,0:T(8,128)(2,1)S(1)}, bf16[32,768]{1,0:T(8,128)(2,1)S(1)}, u32[]{:S(2)}, u32[]{:S(2)}) collective-permute-start(bf16[32,768]{1,0:T(8,128)(2,1)S(1)} %mix.6), channel_id=1, source_target_pairs={{0,4},{2,6},{4,0},{6,2},{8,12},{10,14},{12,8},{14,10},{1,5},{3,7},... | collective-permute-start | bytes 147464 | tf_op jit(solution)/shard_map/ppermute | solution.py:175
  26.5 4.1 %collective-permute-start.5 = (bf16[32,640]{1,0:T(8,128)(2,1)S(1)}, bf16[32,640]{1,0:T(8,128)(2,1)S(1)}, u32[]{:S(2)}, u32[]{:S(2)}) collective-permute-start(bf16[32,640]{1,0:T(8,128)(2,1)S(1)} %mix.5), channel_id=1, source_target_pairs={{0,2},{2,0},{4,6},{6,4},{8,10},{10,8},{12,14},{14,12},{1,3},{3,1},... | collective-permute-start | bytes 122888 | tf_op jit(solution)/shard_map/ppermute | solution.py:175

commit v2 on v1

--- a/solution.py
+++ b/solution.py
@@ -284,11 +284,8 @@
                 latest = [moved(piece, 1, 0, 0) for piece in latest]
                 pieces += latest
 
-        if teams * share > 1:
-            first = len(mates) - len(over_patch)
-            cost = pl.CostEstimate(flops=3000000000, bytes_accessed=10800000, transcendentals=0)
-            found = list(handed_on([*arrived[first:], *pieces], cost_estimate=cost))
-            arrived[first:], pieces = found[: len(over_patch)], found[len(over_patch) :]
+        cost = pl.CostEstimate(flops=500000000, bytes_accessed=1800000, transcendentals=0)
+        pieces = handed_on(pieces, cost_estimate=cost) if pieces else pieces
 
         from_shards = [a for (shift, _), a in zip(mates, arrived) if shift == 0]
         cross_own, *cross_away = call(
@@ -458,6 +455,7 @@
             "weights",
             part_shapes + [pltpu.VMEM((rows, HD), kind)] * len(over_patch),
             sources,
+            cost_estimate=pl.CostEstimate(flops=2000000000, bytes_accessed=7200000, transcendentals=0),
         )
 
         def mixed(spot):

time: 31.5 us -> 30.9 us (0.981)
  waiting for transfers between devices: 8.63 us -> 8.11 us
    ppermute x10, waiting for transfers between devices: 8.63 us -> 8.11 us  [moved(): return lax.ppermute(array, axes, pairs)]
where the time goes in v2:
time: 30.9 us; the launch traced here: 30.7 us
  starting transfers between devices  14.4 us (47%)
  waiting for transfers between devices  8.11 us (26%)
  Pallas kernels  7.5 us (24%)
  between operations  0.71 us (2%)
    ppermute x10, starting transfers between devices, moved(): return lax.ppermute(array, axes, pairs)  14.4 us
    ppermute x10, waiting for transfers between devices, moved(): return lax.ppermute(array, axes, pairs)  8.11 us
    pallas_call x13, Pallas kernels, call(): pl.pallas_call(kernel, out_shape=out_shape, in_specs=[in_spec] * len(oper...  7.5 us
  transfers between devices with their start and end apart: 10, of which 4 were waited for; matrix products, arithmetic and copies ran while one was open for 0% of the time, Pallas kernels for 17%

profile of v2, /device:TPU:0, one launch (start us, length us, event | category | flops | bytes accessed | tf_op | source)
XLA Modules:
  0.0 30.7 jit_solution(16229904521931570130)
XLA Ops:
  0.6 1.6 %pack.1 = (bf16[128,640]{1,0:T(8,128)(2,1)S(1)}, bf16[128,640]{1,0:T(8,128)(2,1)S(1)}, bf16[96,640]{1,0:T(8,128)(2,1)S(1)}, bf16[32,1280]{1,0:T(8,128)(2,1)S(1)}...) custom-call(bf16[1,32,2560]{2,1,0:T(8,128)(2,1)} %query.1, ...), custom_call_target="tpu_custom_call" | custom-call | tf_op jit(solution)/shard_map/pack/pallas_call | solution.py:112
  2.2 5.1 %collective-permute-start.4 = (bf16[128,640]{1,0:T(8,128)(2,1)S(1)}, bf16[128,640]{1,0:T(8,128)(2,1)S(1)}, u32[]{:S(2)}, u32[]{:S(2)}) collective-permute-start(bf16[128,640]{1,0:T(8,128)(2,1)S(1)} %get-tuple-element.38), channel_id=1, source_target_pairs={{0,12},{2,14},{4,8},{6,10},{8,4},{10,6},{12,0},{14,2},{1,13},{3,15... | collective-permute-start | bytes 491528 | tf_op jit(solution)/shard_map/ppermute | solution.py:175
  7.3 0.0 collective-permute-start.3
  7.3 0.6 %collective-permute-start.1 = (bf16[160,640]{1,0:T(8,128)(2,1)S(1)}, bf16[160,640]{1,0:T(8,128)(2,1)S(1)}, u32[]{:S(2)}, u32[]{:S(2)}) collective-permute-start(bf16[160,640]{1,0:T(8,128)(2,1)S(1)} %get-tuple-element.35), channel_id=1, source_target_pairs={{0,4},{2,6},{4,0},{6,2},{8,12},{10,14},{12,8},{14,10},{1,5},{3,7},... | collective-permute-start | bytes 614408 | tf_op jit(solution)/shard_map/ppermute | solution.py:175
  7.9 1.6 %collective-permute-start = (bf16[96,640]{1,0:T(8,128)(2,1)S(1)}, bf16[96,640]{1,0:T(8,128)(2,1)S(1)}, u32[]{:S(2)}, u32[]{:S(2)}) collective-permute-start(bf16[96,640]{1,0:T(8,128)(2,1)S(1)} %get-tuple-element.34), channel_id=1, source_target_pairs={{0,2},{2,0},{4,6},{6,4},{8,10},{10,8},{12,14},{14,12},{1,3},{3,1},... | collective-permute-start | bytes 368648 | tf_op jit(solution)/shard_map/ppermute | solution.py:175
  9.6 0.4 %collective-permute-start.6 = (bf16[32,1280]{1,0:T(8,128)(2,1)S(1)}, bf16[32,1280]{1,0:T(8,128)(2,1)S(1)}, u32[]{:S(2)}, u32[]{:S(2)}) collective-permute-start(bf16[32,1280]{1,0:T(8,128)(2,1)S(1)} %get-tuple-element.47), channel_id=1, source_target_pairs={{0,2},{2,0},{4,6},{6,4},{8,10},{10,8},{12,14},{14,12},{1,3},{3,1},... | collective-permute-start | bytes 245768 | tf_op jit(solution)/shard_map/ppermute | solution.py:175
  10.0 1.7 %load.1 = (bf16[1,512,1280]{2,1,0:T(8,128)(2,1)S(1)}, bf16[1,512,1280]{2,1,0:T(8,128)(2,1)S(1)}, s32[1,512]{1,0:T(1,128)S(1)}) custom-call(bf16[1,512,1280]{2,1,0:T(8,128)(2,1)} %refs_0_.1, bf16[1,512,1280]{2,1,0:T(8,128)(2,1)} %refs_1_.1, s32[1,512]{1,0:T(1,128)} %refs_2_.1), custom_call_target="tpu_custom_call" | custom-call | tf_op jit(solution)/shard_map/load/pallas_call | solution.py:112
  11.7 2.5 %collective-permute-done.6.refs_1_ = bf16[32,1280]{1,0:T(8,128)(2,1)S(1)} collective-permute-done((bf16[32,1280]{1,0:T(8,128)(2,1)S(1)}, bf16[32,1280]{1,0:T(8,128)(2,1)S(1)}, u32[]{:S(2)}, u32[]{:S(2)}) %collective-permute-start.6) | collective-permute-done | bytes 81952 | tf_op jit(solution)/shard_map/ppermute | solution.py:175
  14.2 2.3 %collective-permute-start.2 = (bf16[32,640]{1,0:T(8,128)(2,1)S(1)}, bf16[32,640]{1,0:T(8,128)(2,1)S(1)}, u32[]{:S(2)}, u32[]{:S(2)}) collective-permute-start(bf16[32,640]{1,0:T(8,128)(2,1)S(1)} %get-tuple-element.36), channel_id=1, source_target_pairs={{0,6},{2,4},{4,2},{6,0},{8,14},{10,12},{12,10},{14,8},{1,7},{3,5},... | collective-permute-start | bytes 122888 | tf_op jit(solution)/shard_map/ppermute | solution.py:175
  16.5 0.0 collective-permute-done.refs_1_.refs_3_.refs_6_.refs_4_
  16.5 0.9 %cross.3 = (bf16[32,1280]{1,0:T(8,128)(2,1)S(1)}, bf16[192,640]{1,0:T(8,128)(2,1)S(1)}) custom-call(bf16[32,1280]{1,0:T(8,128)(2,1)S(1)} %get-tuple-element.46.refs_0_, bf16[32,1280]{1,0:T(8,128)(2,1)S(1)} %collective-permute-done.6.refs_1_, bf16[1,512,1280]{2,1,0:T(8,128)(2,1)S(1)} %get-tuple-element.48.refs_2_, ...), custom_call_target="tpu_custom_call" | custom-call | tf_op jit(solution)/shard_map/cross/pallas_call | solution.py:112
  17.4 0.6 %collective-permute-start.7 = (bf16[192,640]{1,0:T(8,128)(2,1)S(1)}, bf16[192,640]{1,0:T(8,128)(2,1)S(1)}, u32[]{:S(2)}, u32[]{:S(2)}) collective-permute-start(bf16[192,640]{1,0:T(8,128)(2,1)S(1)} %get-tuple-element.52), channel_id=1, source_target_pairs={{0,2},{2,0},{4,6},{6,4},{8,10},{10,8},{12,14},{14,12},{1,3},{3,1},... | collective-permute-start | bytes 737288 | tf_op jit(solution)/shard_map/ppermute | solution.py:175
  18.0 0.0 collective-permute-done.4.refs_1_
  18.0 3.3 %collective-permute-done.3.refs_0_ = bf16[128,640]{1,0:T(8,128)(2,1)S(1)} collective-permute-done((bf16[128,640]{1,0:T(8,128)(2,1)S(1)}, bf16[128,640]{1,0:T(8,128)(2,1)S(1)}, u32[]{:S(2)}, u32[]{:S(2)}) %collective-permute-start.3) | collective-permute-done | bytes 163872 | tf_op jit(solution)/shard_map/ppermute | solution.py:175
  21.3 0.0 collective-permute-done.2.refs_3_.refs_5_.refs_6_
  21.3 0.0 collective-permute-done.1.refs_2_.refs_4_.refs_5_
  21.3 0.6 %weights.1 = (bf16[5,32,256]{2,1,0:T(8,128)(2,1)S(1)}, f32[5,32,128]{2,1,0:T(8,128)S(1)}, bf16[5,32,256]{2,1,0:T(8,128)(2,1)S(1)}, f32[5,32,128]{2,1,0:T(8,128)S...) custom-call(bf16[96,640]{1,0:T(8,128)(2,1)S(1)} %get-tuple-element.3, ...), custom_call_target="tpu_custom_call" | custom-call | flops 2000000000 | bytes 7200000 | tf_op jit(solution)/shard_map/weights/pallas_call | solution.py:112
  21.9 0.2 mix.7
  22.1 1.9 %collective-permute-start.9 = (bf16[32,768]{1,0:T(8,128)(2,1)S(1)}, bf16[32,768]{1,0:T(8,128)(2,1)S(1)}, u32[]{:S(2)}, u32[]{:S(2)}) collective-permute-start(bf16[32,768]{1,0:T(8,128)(2,1)S(1)} %mix.7), channel_id=1, source_target_pairs={{0,6},{2,4},{4,2},{6,0},{8,14},{10,12},{12,10},{14,8},{1,7},{3,5},... | collective-permute-start | bytes 147464 | tf_op jit(solution)/shard_map/ppermute | solution.py:175
  24.0 0.2 mix.6
  24.1 1.6 %collective-permute-start.8 = (bf16[32,768]{1,0:T(8,128)(2,1)S(1)}, bf16[32,768]{1,0:T(8,128)(2,1)S(1)}, u32[]{:S(2)}, u32[]{:S(2)}) collective-permute-start(bf16[32,768]{1,0:T(8,128)(2,1)S(1)} %mix.6), channel_id=1, source_target_pairs={{0,4},{2,6},{4,0},{6,2},{8,12},{10,14},{12,8},{14,10},{1,5},{3,7},... | collective-permute-start | bytes 147464 | tf_op jit(solution)/shard_map/ppermute | solution.py:175
  25.7 0.2 mix.5
  25.9 0.2 collective-permute-start.5
  26.1 0.2 mix.4.refs_0_
  26.3 0.0 collective-permute-done.7.refs_1_
  26.3 0.7 %place_cross.1 = bf16[1,32,2560]{2,1,0:T(8,128)(2,1)} custom-call(bf16[32,1280]{1,0:T(8,128)(2,1)S(1)} %get-tuple-element.63.refs_0_, bf16[192,640]{1,0:T(8,128)(2,1)S(1)} %collective-permute-done.7.refs_1_), custom_call_target="tpu_custom_call" | custom-call | tf_op jit(solution)/shard_map/place_cross/pallas_call | solution.py:112
  27.0 0.4 %near.1 = (f32[32,1280]{1,0:T(8,128)S(1)}, f32[10,32,128]{2,1,0:T(8,128)S(1)}) custom-call(bf16[192,640]{1,0:T(8,128)(2,1)S(1)} %get-tuple-element.45.refs_0_, bf16[192,640]{1,0:T(8,128)(2,1)S(1)} %collective-permute-done.7.refs_1_), custom_call_target="tpu_custom_call" | custom-call | tf_op jit(solution)/shard_map/near/pallas_call | solution.py:112
  27.4 0.0 collective-permute-done.9.refs_3_
  27.4 0.8 %collective-permute-done.8.refs_2_ = bf16[32,768]{1,0:T(8,128)(2,1)S(1)} collective-permute-done((bf16[32,768]{1,0:T(8,128)(2,1)S(1)}, bf16[32,768]{1,0:T(8,128)(2,1)S(1)}, u32[]{:S(2)}, u32[]{:S(2)}) %collective-permute-start.8) | collective-permute-done | bytes 49184 | tf_op jit(solution)/shard_map/ppermute | solution.py:175
  28.3 0.2 merge.1
  28.5 1.5 %collective-permute-done.5.refs_1_ = bf16[32,640]{1,0:T(8,128)(2,1)S(1)} collective-permute-done((bf16[32,640]{1,0:T(8,128)(2,1)S(1)}, bf16[32,640]{1,0:T(8,128)(2,1)S(1)}, u32[]{:S(2)}, u32[]{:S(2)}) %collective-permute-start.5) | collective-permute-done | bytes 40992 | tf_op jit(solution)/shard_map/ppermute | solution.py:175
  30.0 0.7 %place_self.1 = bf16[1,32,2560]{2,1,0:T(8,128)(2,1)} custom-call(bf16[32,640]{1,0:T(8,128)(2,1)S(1)} %mix.4.refs_0_, bf16[32,640]{1,0:T(8,128)(2,1)S(1)} %collective-permute-done.5.refs_1_, bf16[32,640]{1,0:T(8,128)(2,1)S(1)} %get-tuple-element.61.refs_2_, bf16[32,640]{1,0:T(8,128)(2,1)S(1)} %get-tuple-element.62.refs_3_), custom_call_target="tpu_custom_call" | custom-call | tf_op jit(solution)/shard_map/place_self/pallas_call | solution.py:112
  (1 shorter events, 0.0 us)
Async XLA Ops:
  2.2 15.8 %collective-permute-start.4 = (bf16[128,640]{1,0:T(8,128)(2,1)S(1)}, bf16[128,640]{1,0:T(8,128)(2,1)S(1)}, u32[]{:S(2)}, u32[]{:S(2)}) collective-permute-start(bf16[128,640]{1,0:T(8,128)(2,1)S(1)} %get-tuple-element.38), channel_id=1, source_target_pairs={{0,12},{2,14},{4,8},{6,10},{8,4},{10,6},{12,0},{14,2},{1,13},{3,15... | collective-permute-start | bytes 491528 | tf_op jit(solution)/shard_map/ppermute | solution.py:175
  7.3 14.0 %collective-permute-start.3 = (bf16[128,640]{1,0:T(8,128)(2,1)S(1)}, bf16[128,640]{1,0:T(8,128)(2,1)S(1)}, u32[]{:S(2)}, u32[]{:S(2)}) collective-permute-start(bf16[128,640]{1,0:T(8,128)(2,1)S(1)} %get-tuple-element.37.refs_4_.refs_6_.refs_7_), channel_id=1, source_target_pairs={{0,8},{2,10},{4,12},{6,14},{8,0},{10,2},{12,4},{14,6},{1,9},{3,11}... | collective-permute-start | bytes 491528 | tf_op jit(solution)/shard_map/ppermute | solution.py:175
  7.3 14.0 %collective-permute-start.1 = (bf16[160,640]{1,0:T(8,128)(2,1)S(1)}, bf16[160,640]{1,0:T(8,128)(2,1)S(1)}, u32[]{:S(2)}, u32[]{:S(2)}) collective-permute-start(bf16[160,640]{1,0:T(8,128)(2,1)S(1)} %get-tuple-element.35), channel_id=1, source_target_pairs={{0,4},{2,6},{4,0},{6,2},{8,12},{10,14},{12,8},{14,10},{1,5},{3,7},... | collective-permute-start | bytes 614408 | tf_op jit(solution)/shard_map/ppermute | solution.py:175
  7.9 8.6 %collective-permute-start = (bf16[96,640]{1,0:T(8,128)(2,1)S(1)}, bf16[96,640]{1,0:T(8,128)(2,1)S(1)}, u32[]{:S(2)}, u32[]{:S(2)}) collective-permute-start(bf16[96,640]{1,0:T(8,128)(2,1)S(1)} %get-tuple-element.34), channel_id=1, source_target_pairs={{0,2},{2,0},{4,6},{6,4},{8,10},{10,8},{12,14},{14,12},{1,3},{3,1},... | collective-permute-start | bytes 368648 | tf_op jit(solution)/shard_map/ppermute | solution.py:175
  9.6 4.6 %collective-permute-start.6 = (bf16[32,1280]{1,0:T(8,128)(2,1)S(1)}, bf16[32,1280]{1,0:T(8,128)(2,1)S(1)}, u32[]{:S(2)}, u32[]{:S(2)}) collective-permute-start(bf16[32,1280]{1,0:T(8,128)(2,1)S(1)} %get-tuple-element.47), channel_id=1, source_target_pairs={{0,2},{2,0},{4,6},{6,4},{8,10},{10,8},{12,14},{14,12},{1,3},{3,1},... | collective-permute-start | bytes 245768 | tf_op jit(solution)/shard_map/ppermute | solution.py:175
  14.2 7.1 %collective-permute-start.2 = (bf16[32,640]{1,0:T(8,128)(2,1)S(1)}, bf16[32,640]{1,0:T(8,128)(2,1)S(1)}, u32[]{:S(2)}, u32[]{:S(2)}) collective-permute-start(bf16[32,640]{1,0:T(8,128)(2,1)S(1)} %get-tuple-element.36), channel_id=1, source_target_pairs={{0,6},{2,4},{4,2},{6,0},{8,14},{10,12},{12,10},{14,8},{1,7},{3,5},... | collective-permute-start | bytes 122888 | tf_op jit(solution)/shard_map/ppermute | solution.py:175
  17.4 8.9 %collective-permute-start.7 = (bf16[192,640]{1,0:T(8,128)(2,1)S(1)}, bf16[192,640]{1,0:T(8,128)(2,1)S(1)}, u32[]{:S(2)}, u32[]{:S(2)}) collective-permute-start(bf16[192,640]{1,0:T(8,128)(2,1)S(1)} %get-tuple-element.52), channel_id=1, source_target_pairs={{0,2},{2,0},{4,6},{6,4},{8,10},{10,8},{12,14},{14,12},{1,3},{3,1},... | collective-permute-start | bytes 737288 | tf_op jit(solution)/shard_map/ppermute | solution.py:175
  22.1 5.4 %collective-permute-start.9 = (bf16[32,768]{1,0:T(8,128)(2,1)S(1)}, bf16[32,768]{1,0:T(8,128)(2,1)S(1)}, u32[]{:S(2)}, u32[]{:S(2)}) collective-permute-start(bf16[32,768]{1,0:T(8,128)(2,1)S(1)} %mix.7), channel_id=1, source_target_pairs={{0,6},{2,4},{4,2},{6,0},{8,14},{10,12},{12,10},{14,8},{1,7},{3,5},... | collective-permute-start | bytes 147464 | tf_op jit(solution)/shard_map/ppermute | solution.py:175
  24.1 4.1 %collective-permute-start.8 = (bf16[32,768]{1,0:T(8,128)(2,1)S(1)}, bf16[32,768]{1,0:T(8,128)(2,1)S(1)}, u32[]{:S(2)}, u32[]{:S(2)}) collective-permute-start(bf16[32,768]{1,0:T(8,128)(2,1)S(1)} %mix.6), channel_id=1, source_target_pairs={{0,4},{2,6},{4,0},{6,2},{8,12},{10,14},{12,8},{14,10},{1,5},{3,7},... | collective-permute-start | bytes 147464 | tf_op jit(solution)/shard_map/ppermute | solution.py:175
  25.9 4.1 %collective-permute-start.5 = (bf16[32,640]{1,0:T(8,128)(2,1)S(1)}, bf16[32,640]{1,0:T(8,128)(2,1)S(1)}, u32[]{:S(2)}, u32[]{:S(2)}) collective-permute-start(bf16[32,640]{1,0:T(8,128)(2,1)S(1)} %mix.5), channel_id=1, source_target_pairs={{0,2},{2,0},{4,6},{6,4},{8,10},{10,8},{12,14},{14,12},{1,3},{3,1},... | collective-permute-start | bytes 122888 | tf_op jit(solution)/shard_map/ppermute | solution.py:175

commit v3 on v0

--- a/solution.py
+++ b/solution.py
@@ -185,19 +185,34 @@
         def message_rows(shift, turn):
             return fresh_start(shift, turn) + (3 if shift == 0 else 1) * rows
 
+        def stale_copies(shift, sources, target):
+            part = lax.rem(lax.axis_index("patch") + shift, share)
+            lanes = pl.ds(pl.multiple_of(part * width, HD), width)
+            return [
+                (source.at[0, :, lanes], target.at[pl.ds(index * patch_rows, patch_rows)])
+                for index, source in enumerate(sources)
+            ]
+
+        def stale_kernel(*refs):
+            copies = []
+            for shift in range(share):
+                copies += stale_copies(shift, refs[:2], refs[2 + shift])
+            run_all(copies, refs[-1])
+
+        stale = call(
+            stale_kernel,
+            "pack_stale",
+            [pltpu.VMEM((stale_rows, width), kind)] * share,
+            in_hbm(stale_key, stale_value),
+            in_spec=hbm,
+            scratch=[pltpu.SemaphoreType.DMA((2 * share,))],
+        )
+
         def pack_kernel(query, key, value, old_key, old_value, cross, *refs):
-            stale, own, refs = refs[:share], refs[share], refs[share + 1 :]
+            own, refs = refs[0], refs[1:]
             crosses, messages = refs[:shards], refs[shards : shards + len(mates)]
             nears = refs[shards + len(mates) : -1]
-            me = lax.rem(lax.axis_index("patch"), share)
             copies = []
-
-            def stale_copies(shift, target):
-                part = lax.rem(me + shift, share)
-                lanes = pl.ds(pl.multiple_of(part * width, HD), width)
-                for index, source in enumerate((old_key, old_value)):
-                    block = pl.ds(index * patch_rows, patch_rows)
-                    copies.append((source.at[0, :, lanes], target.at[block]))
 
             def fresh_copies(shift, turn, target, first):
                 for index, source in enumerate((query, key, value)[: 3 if shift == 0 else 1]):
@@ -207,10 +222,8 @@
             for (shift, turn), message in zip(mates, messages):
                 first = fresh_start(shift, turn)
                 if first:
-                    stale_copies(shift, message)
+                    copies.extend(stale_copies(shift, (old_key, old_value), message))
                 fresh_copies(shift, turn, message, first)
-            for shift in range(share):
-                stale_copies(shift, stale[shift])
             fresh_copies(0, 0, own, 0)
             for turn, target in enumerate(crosses):
                 shard = lax.rem(lax.axis_index("head") + turn, shards)
@@ -224,14 +237,13 @@
             run_all(copies, refs[-1])
 
         packed_shapes = (
-            [(stale_rows, width)] * share
-            + [(3 * rows, width)]
+            [(3 * rows, width)]
             + [(rows, cols)] * shards
             + [(message_rows(*mate), width) for mate in mates]
         )
         if near_blocks:
             packed_shapes += [(3 * rows, near_width)] + [(2 * rows, near_width)] * (shards - 1)
-        copy_count = 2 * share + 3 + shards + sum(
+        copy_count = 3 + shards + sum(
             (3 if mate[0] == 0 else 1) + (2 if fresh_start(*mate) else 0) for mate in mates
         )
         copy_count += len(near_blocks) * (2 * shards + 1)
@@ -243,7 +255,7 @@
             in_spec=hbm,
             scratch=[pltpu.SemaphoreType.DMA((copy_count,))],
         )
-        stale, own, packed = packed[:share], packed[share], packed[share + 1 :]
+        own, packed = packed[0], packed[1:]
         crosses, messages = packed[:shards], packed[shards : shards + len(mates)]
         nears = packed[shards + len(mates) :]
         text = [text_key, text_value, text_mask]

time: 30.8 us -> 30.3 us (0.984)
  waiting for transfers between devices: 6.56 us -> 5.31 us
  Pallas kernels: 7.51 us -> 8.41 us
    ppermute x11, waiting for transfers between devices: 6.56 us -> 5.31 us  [moved(): return lax.ppermute(array, axes, pairs)]
    pallas_call x14 -> x15, Pallas kernels: 7.51 us -> 8.41 us  [call(): pl.pallas_call(kernel, out_shape=out_shape, in_specs=[in_spec] * len(oper...]
  transfers between devices with their start and end apart: 11 -> 11, of which waited for: 5 -> 6; matrix products, arithmetic and copies ran while one was open for 0% -> 0% of each run, Pallas kernels for 17% -> 22%
where the time goes in v3:
time: 30.3 us; the launch traced here: 30.1 us
  starting transfers between devices  15.6 us (51%)
  Pallas kernels  8.41 us (28%)
  waiting for transfers between devices  5.31 us (18%)
  between operations  0.74 us (2%)
    ppermute x11, starting transfers between devices, moved(): return lax.ppermute(array, axes, pairs)  15.6 us
    pallas_call x15, Pallas kernels, call(): pl.pallas_call(kernel, out_shape=out_shape, in_specs=[in_spec] * len(oper...  8.41 us
    ppermute x11, waiting for transfers between devices, moved(): return lax.ppermute(array, axes, pairs)  5.31 us
  transfers between devices with their start and end apart: 11, of which 6 were waited for; matrix products, arithmetic and copies ran while one was open for 0% of the time, Pallas kernels for 22%

profile of v3, /device:TPU:0, one launch (start us, length us, event | category | flops | bytes accessed | tf_op | source)
XLA Modules:
  0.0 30.1 jit_solution(6185870949661786565)
XLA Ops:
  0.6 1.1 %pack_stale.1 = (bf16[128,640]{1,0:T(8,128)(2,1)S(1)}, bf16[128,640]{1,0:T(8,128)(2,1)S(1)}) custom-call(bf16[1,64,1280]{2,1,0:T(8,128)(2,1)} %refs_0_.2, bf16[1,64,1280]{2,1,0:T(8,128)(2,1)} %refs_1_.2), custom_call_target="tpu_custom_call" | custom-call | tf_op jit(solution)/shard_map/pack_stale/pallas_call | solution.py:106
  1.7 5.1 %collective-permute-start.4 = (bf16[128,640]{1,0:T(8,128)(2,1)S(1)}, bf16[128,640]{1,0:T(8,128)(2,1)S(1)}, u32[]{:S(2)}, u32[]{:S(2)}) collective-permute-start(bf16[128,640]{1,0:T(8,128)(2,1)S(1)} %get-tuple-element.38), channel_id=1, source_target_pairs={{0,12},{2,14},{4,8},{6,10},{8,4},{10,6},{12,0},{14,2},{1,13},{3,15... | collective-permute-start | bytes 491528 | tf_op jit(solution)/shard_map/ppermute | solution.py:169
  6.8 0.0 collective-permute-start.3
  6.8 1.4 %pack.1 = (bf16[96,640]{1,0:T(8,128)(2,1)S(1)}, bf16[32,1280]{1,0:T(8,128)(2,1)S(1)}, bf16[32,1280]{1,0:T(8,128)(2,1)S(1)}, bf16[96,640]{1,0:T(8,128)(2,1)S(1)},...) custom-call(bf16[1,32,2560]{2,1,0:T(8,128)(2,1)} %query.1, ...), custom_call_target="tpu_custom_call" | custom-call | tf_op jit(solution)/shard_map/pack/pallas_call | solution.py:106
  8.2 0.7 %collective-permute-start.1 = (bf16[160,640]{1,0:T(8,128)(2,1)S(1)}, bf16[160,640]{1,0:T(8,128)(2,1)S(1)}, u32[]{:S(2)}, u32[]{:S(2)}) collective-permute-start(bf16[160,640]{1,0:T(8,128)(2,1)S(1)} %get-tuple-element.35), channel_id=1, source_target_pairs={{0,4},{2,6},{4,0},{6,2},{8,12},{10,14},{12,8},{14,10},{1,5},{3,7},... | collective-permute-start | bytes 614408 | tf_op jit(solution)/shard_map/ppermute | solution.py:169
  8.9 1.6 %collective-permute-start.9 = (bf16[32,1280]{1,0:T(8,128)(2,1)S(1)}, bf16[32,1280]{1,0:T(8,128)(2,1)S(1)}, u32[]{:S(2)}, u32[]{:S(2)}) collective-permute-start(bf16[32,1280]{1,0:T(8,128)(2,1)S(1)} %get-tuple-element.59), channel_id=1, source_target_pairs={{0,2},{2,0},{4,6},{6,4},{8,10},{10,8},{12,14},{14,12},{1,3},{3,1},... | collective-permute-start | bytes 245768 | tf_op jit(solution)/shard_map/ppermute | solution.py:169
  10.6 0.4 %collective-permute-start = (bf16[96,640]{1,0:T(8,128)(2,1)S(1)}, bf16[96,640]{1,0:T(8,128)(2,1)S(1)}, u32[]{:S(2)}, u32[]{:S(2)}) collective-permute-start(bf16[96,640]{1,0:T(8,128)(2,1)S(1)} %get-tuple-element.34), channel_id=1, source_target_pairs={{0,2},{2,0},{4,6},{6,4},{8,10},{10,8},{12,14},{14,12},{1,3},{3,1},... | collective-permute-start | bytes 368648 | tf_op jit(solution)/shard_map/ppermute | solution.py:169
  10.9 1.7 %load.1 = (bf16[1,512,1280]{2,1,0:T(8,128)(2,1)S(1)}, bf16[1,512,1280]{2,1,0:T(8,128)(2,1)S(1)}, s32[1,512]{1,0:T(1,128)S(1)}) custom-call(bf16[1,512,1280]{2,1,0:T(8,128)(2,1)} %refs_0_.3, bf16[1,512,1280]{2,1,0:T(8,128)(2,1)} %refs_1_.3, s32[1,512]{1,0:T(1,128)} %refs_2_.1), custom_call_target="tpu_custom_call" | custom-call | tf_op jit(solution)/shard_map/load/pallas_call | solution.py:106
  12.7 1.5 %collective-permute-done.9.refs_1_ = bf16[32,1280]{1,0:T(8,128)(2,1)S(1)} collective-permute-done((bf16[32,1280]{1,0:T(8,128)(2,1)S(1)}, bf16[32,1280]{1,0:T(8,128)(2,1)S(1)}, u32[]{:S(2)}, u32[]{:S(2)}) %collective-permute-start.9) | collective-permute-done | bytes 81952 | tf_op jit(solution)/shard_map/ppermute | solution.py:169
  14.2 1.2 %collective-permute-start.6 = (bf16[64,1280]{1,0:T(8,128)(2,1)S(1)}, bf16[64,1280]{1,0:T(8,128)(2,1)S(1)}, u32[]{:S(2)}, u32[]{:S(2)}) collective-permute-start(bf16[64,1280]{1,0:T(8,128)(2,1)S(1)} %gate.3), channel_id=1, source_target_pairs={{0,2},{2,0},{4,6},{6,4},{8,10},{10,8},{12,14},{14,12},{1,3},{3,1},... | collective-permute-start | bytes 491528 | tf_op jit(solution)/shard_map/ppermute | solution.py:169
  15.3 1.2 %collective-permute-done.refs_1_.refs_3_.refs_4_.refs_5_ = bf16[96,640]{1,0:T(8,128)(2,1)S(1)} collective-permute-done((bf16[96,640]{1,0:T(8,128)(2,1)S(1)}, bf16[96,640]{1,0:T(8,128)(2,1)S(1)}, u32[]{:S(2)}, u32[]{:S(2)}) %collective-permute-start) | collective-permute-done | bytes 122912 | tf_op jit(solution)/shard_map/ppermute | solution.py:169
  16.6 1.6 %collective-permute-start.2 = (bf16[32,640]{1,0:T(8,128)(2,1)S(1)}, bf16[32,640]{1,0:T(8,128)(2,1)S(1)}, u32[]{:S(2)}, u32[]{:S(2)}) collective-permute-start(bf16[32,640]{1,0:T(8,128)(2,1)S(1)} %get-tuple-element.36), channel_id=1, source_target_pairs={{0,6},{2,4},{4,2},{6,0},{8,14},{10,12},{12,10},{14,8},{1,7},{3,5},... | collective-permute-start | bytes 122888 | tf_op jit(solution)/shard_map/ppermute | solution.py:169
  18.2 0.9 %cross.3 = (bf16[32,1280]{1,0:T(8,128)(2,1)S(1)}, bf16[32,1280]{1,0:T(8,128)(2,1)S(1)}) custom-call(bf16[32,1280]{1,0:T(8,128)(2,1)S(1)} %get-tuple-element.58.refs_0_, bf16[32,1280]{1,0:T(8,128)(2,1)S(1)} %collective-permute-done.9.refs_1_, bf16[1,512,1280]{2,1,0:T(8,128)(2,1)S(1)} %get-tuple-element.60.refs_2_, ...), custom_call_target="tpu_custom_call" | custom-call | tf_op jit(solution)/shard_map/cross/pallas_call | solution.py:106
  19.1 0.0 collective-permute-done.4.refs_1_
  19.1 1.3 %collective-permute-start.10 = (bf16[32,1280]{1,0:T(8,128)(2,1)S(1)}, bf16[32,1280]{1,0:T(8,128)(2,1)S(1)}, u32[]{:S(2)}, u32[]{:S(2)}) collective-permute-start(bf16[32,1280]{1,0:T(8,128)(2,1)S(1)} %get-tuple-element.63), channel_id=1, source_target_pairs={{0,2},{2,0},{4,6},{6,4},{8,10},{10,8},{12,14},{14,12},{1,3},{3,1},... | collective-permute-start | bytes 245768 | tf_op jit(solution)/shard_map/ppermute | solution.py:169
  20.4 0.3 %collective-permute-done.3.refs_0_ = bf16[128,640]{1,0:T(8,128)(2,1)S(1)} collective-permute-done((bf16[128,640]{1,0:T(8,128)(2,1)S(1)}, bf16[128,640]{1,0:T(8,128)(2,1)S(1)}, u32[]{:S(2)}, u32[]{:S(2)}) %collective-permute-start.3) | collective-permute-done | bytes 163872 | tf_op jit(solution)/shard_map/ppermute | solution.py:169
  20.7 1.3 %collective-permute-done.2.refs_3_.refs_5_.refs_6_ = bf16[32,640]{1,0:T(8,128)(2,1)S(1)} collective-permute-done((bf16[32,640]{1,0:T(8,128)(2,1)S(1)}, bf16[32,640]{1,0:T(8,128)(2,1)S(1)}, u32[]{:S(2)}, u32[]{:S(2)}) %collective-permute-start.2) | collective-permute-done | bytes 40992 | tf_op jit(solution)/shard_map/ppermute | solution.py:169
  22.1 0.0 collective-permute-done.1.refs_2_.refs_4_.refs_5_
  22.1 0.6 %weights.1 = (bf16[5,32,256]{2,1,0:T(8,128)(2,1)S(1)}, f32[5,32,128]{2,1,0:T(8,128)S(1)}, bf16[5,32,256]{2,1,0:T(8,128)(2,1)S(1)}, f32[5,32,128]{2,1,0:T(8,128)S...) custom-call(bf16[96,640]{1,0:T(8,128)(2,1)S(1)} %get-tuple-element.3, ...), custom_call_target="tpu_custom_call" | custom-call | tf_op jit(solution)/shard_map/weights/pallas_call | solution.py:106
  22.6 0.2 mix.7
  22.8 1.2 %collective-permute-start.8 = (bf16[32,768]{1,0:T(8,128)(2,1)S(1)}, bf16[32,768]{1,0:T(8,128)(2,1)S(1)}, u32[]{:S(2)}, u32[]{:S(2)}) collective-permute-start(bf16[32,768]{1,0:T(8,128)(2,1)S(1)} %mix.7), channel_id=1, source_target_pairs={{0,6},{2,4},{4,2},{6,0},{8,14},{10,12},{12,10},{14,8},{1,7},{3,5},... | collective-permute-start | bytes 147464 | tf_op jit(solution)/shard_map/ppermute | solution.py:169
  24.1 0.2 mix.6
  24.3 0.9 %collective-permute-start.7 = (bf16[32,768]{1,0:T(8,128)(2,1)S(1)}, bf16[32,768]{1,0:T(8,128)(2,1)S(1)}, u32[]{:S(2)}, u32[]{:S(2)}) collective-permute-start(bf16[32,768]{1,0:T(8,128)(2,1)S(1)} %mix.6), channel_id=1, source_target_pairs={{0,4},{2,6},{4,0},{6,2},{8,12},{10,14},{12,8},{14,10},{1,5},{3,7},... | collective-permute-start | bytes 147464 | tf_op jit(solution)/shard_map/ppermute | solution.py:169
  25.1 0.2 mix.5
  25.3 1.6 %collective-permute-start.5 = (bf16[32,640]{1,0:T(8,128)(2,1)S(1)}, bf16[32,640]{1,0:T(8,128)(2,1)S(1)}, u32[]{:S(2)}, u32[]{:S(2)}) collective-permute-start(bf16[32,640]{1,0:T(8,128)(2,1)S(1)} %mix.5), channel_id=1, source_target_pairs={{0,2},{2,0},{4,6},{6,4},{8,10},{10,8},{12,14},{14,12},{1,3},{3,1},... | collective-permute-start | bytes 122888 | tf_op jit(solution)/shard_map/ppermute | solution.py:169
  26.9 0.0 collective-permute-done.6.refs_1_
  26.9 0.4 %near.1 = (f32[32,1280]{1,0:T(8,128)S(1)}, f32[10,32,128]{2,1,0:T(8,128)S(1)}) custom-call(bf16[96,1280]{1,0:T(8,128)(2,1)S(1)} %get-tuple-element.45.refs_0_, bf16[64,1280]{1,0:T(8,128)(2,1)S(1)} %collective-permute-done.6.refs_1_), custom_call_target="tpu_custom_call" | custom-call | tf_op jit(solution)/shard_map/near/pallas_call | solution.py:106
  27.3 0.2 mix.4.refs_0_
  27.5 0.0 collective-permute-done.10.refs_1_
  27.5 0.7 %place_cross.1 = bf16[1,32,2560]{2,1,0:T(8,128)(2,1)} custom-call(bf16[32,1280]{1,0:T(8,128)(2,1)S(1)} %get-tuple-element.62.refs_0_, bf16[32,1280]{1,0:T(8,128)(2,1)S(1)} %collective-permute-done.10.refs_1_), custom_call_target="tpu_custom_call" | custom-call | tf_op jit(solution)/shard_map/place_cross/pallas_call | solution.py:106
  28.2 0.0 collective-permute-done.8.refs_3_
  28.2 0.2 collective-permute-done.7.refs_2_
  28.4 0.2 merge.1
  28.6 0.8 %collective-permute-done.5.refs_1_ = bf16[32,640]{1,0:T(8,128)(2,1)S(1)} collective-permute-done((bf16[32,640]{1,0:T(8,128)(2,1)S(1)}, bf16[32,640]{1,0:T(8,128)(2,1)S(1)}, u32[]{:S(2)}, u32[]{:S(2)}) %collective-permute-start.5) | collective-permute-done | bytes 40992 | tf_op jit(solution)/shard_map/ppermute | solution.py:169
  29.4 0.7 %place_self.1 = bf16[1,32,2560]{2,1,0:T(8,128)(2,1)} custom-call(bf16[32,640]{1,0:T(8,128)(2,1)S(1)} %mix.4.refs_0_, bf16[32,640]{1,0:T(8,128)(2,1)S(1)} %collective-permute-done.5.refs_1_, bf16[32,640]{1,0:T(8,128)(2,1)S(1)} %get-tuple-element.56.refs_2_, bf16[32,640]{1,0:T(8,128)(2,1)S(1)} %get-tuple-element.57.refs_3_), custom_call_target="tpu_custom_call" | custom-call | tf_op jit(solution)/shard_map/place_self/pallas_call | solution.py:106
  (2 shorter events, 0.0 us)
Async XLA Ops:
  1.7 17.4 %collective-permute-start.4 = (bf16[128,640]{1,0:T(8,128)(2,1)S(1)}, bf16[128,640]{1,0:T(8,128)(2,1)S(1)}, u32[]{:S(2)}, u32[]{:S(2)}) collective-permute-start(bf16[128,640]{1,0:T(8,128)(2,1)S(1)} %get-tuple-element.38), channel_id=1, source_target_pairs={{0,12},{2,14},{4,8},{6,10},{8,4},{10,6},{12,0},{14,2},{1,13},{3,15... | collective-permute-start | bytes 491528 | tf_op jit(solution)/shard_map/ppermute | solution.py:169
  6.8 13.9 %collective-permute-start.3 = (bf16[128,640]{1,0:T(8,128)(2,1)S(1)}, bf16[128,640]{1,0:T(8,128)(2,1)S(1)}, u32[]{:S(2)}, u32[]{:S(2)}) collective-permute-start(bf16[128,640]{1,0:T(8,128)(2,1)S(1)} %get-tuple-element.37.refs_4_.refs_6_.refs_7_), channel_id=1, source_target_pairs={{0,8},{2,10},{4,12},{6,14},{8,0},{10,2},{12,4},{14,6},{1,9},{3,11}... | collective-permute-start | bytes 491528 | tf_op jit(solution)/shard_map/ppermute | solution.py:169
  8.2 13.8 %collective-permute-start.1 = (bf16[160,640]{1,0:T(8,128)(2,1)S(1)}, bf16[160,640]{1,0:T(8,128)(2,1)S(1)}, u32[]{:S(2)}, u32[]{:S(2)}) collective-permute-start(bf16[160,640]{1,0:T(8,128)(2,1)S(1)} %get-tuple-element.35), channel_id=1, source_target_pairs={{0,4},{2,6},{4,0},{6,2},{8,12},{10,14},{12,8},{14,10},{1,5},{3,7},... | collective-permute-start | bytes 614408 | tf_op jit(solution)/shard_map/ppermute | solution.py:169
  8.9 5.2 %collective-permute-start.9 = (bf16[32,1280]{1,0:T(8,128)(2,1)S(1)}, bf16[32,1280]{1,0:T(8,128)(2,1)S(1)}, u32[]{:S(2)}, u32[]{:S(2)}) collective-permute-start(bf16[32,1280]{1,0:T(8,128)(2,1)S(1)} %get-tuple-element.59), channel_id=1, source_target_pairs={{0,2},{2,0},{4,6},{6,4},{8,10},{10,8},{12,14},{14,12},{1,3},{3,1},... | collective-permute-start | bytes 245768 | tf_op jit(solution)/shard_map/ppermute | solution.py:169
  10.6 6.0 %collective-permute-start = (bf16[96,640]{1,0:T(8,128)(2,1)S(1)}, bf16[96,640]{1,0:T(8,128)(2,1)S(1)}, u32[]{:S(2)}, u32[]{:S(2)}) collective-permute-start(bf16[96,640]{1,0:T(8,128)(2,1)S(1)} %get-tuple-element.34), channel_id=1, source_target_pairs={{0,2},{2,0},{4,6},{6,4},{8,10},{10,8},{12,14},{14,12},{1,3},{3,1},... | collective-permute-start | bytes 368648 | tf_op jit(solution)/shard_map/ppermute | solution.py:169
  14.2 12.7 %collective-permute-start.6 = (bf16[64,1280]{1,0:T(8,128)(2,1)S(1)}, bf16[64,1280]{1,0:T(8,128)(2,1)S(1)}, u32[]{:S(2)}, u32[]{:S(2)}) collective-permute-start(bf16[64,1280]{1,0:T(8,128)(2,1)S(1)} %gate.3), channel_id=1, source_target_pairs={{0,2},{2,0},{4,6},{6,4},{8,10},{10,8},{12,14},{14,12},{1,3},{3,1},... | collective-permute-start | bytes 491528 | tf_op jit(solution)/shard_map/ppermute | solution.py:169
  16.6 5.5 %collective-permute-start.2 = (bf16[32,640]{1,0:T(8,128)(2,1)S(1)}, bf16[32,640]{1,0:T(8,128)(2,1)S(1)}, u32[]{:S(2)}, u32[]{:S(2)}) collective-permute-start(bf16[32,640]{1,0:T(8,128)(2,1)S(1)} %get-tuple-element.36), channel_id=1, source_target_pairs={{0,6},{2,4},{4,2},{6,0},{8,14},{10,12},{12,10},{14,8},{1,7},{3,5},... | collective-permute-start | bytes 122888 | tf_op jit(solution)/shard_map/ppermute | solution.py:169
  19.1 8.4 %collective-permute-start.10 = (bf16[32,1280]{1,0:T(8,128)(2,1)S(1)}, bf16[32,1280]{1,0:T(8,128)(2,1)S(1)}, u32[]{:S(2)}, u32[]{:S(2)}) collective-permute-start(bf16[32,1280]{1,0:T(8,128)(2,1)S(1)} %get-tuple-element.63), channel_id=1, source_target_pairs={{0,2},{2,0},{4,6},{6,4},{8,10},{10,8},{12,14},{14,12},{1,3},{3,1},... | collective-permute-start | bytes 245768 | tf_op jit(solution)/shard_map/ppermute | solution.py:169
  22.8 5.4 %collective-permute-start.8 = (bf16[32,768]{1,0:T(8,128)(2,1)S(1)}, bf16[32,768]{1,0:T(8,128)(2,1)S(1)}, u32[]{:S(2)}, u32[]{:S(2)}) collective-permute-start(bf16[32,768]{1,0:T(8,128)(2,1)S(1)} %mix.7), channel_id=1, source_target_pairs={{0,6},{2,4},{4,2},{6,0},{8,14},{10,12},{12,10},{14,8},{1,7},{3,5},... | collective-permute-start | bytes 147464 | tf_op jit(solution)/shard_map/ppermute | solution.py:169
  24.3 4.1 %collective-permute-start.7 = (bf16[32,768]{1,0:T(8,128)(2,1)S(1)}, bf16[32,768]{1,0:T(8,128)(2,1)S(1)}, u32[]{:S(2)}, u32[]{:S(2)}) collective-permute-start(bf16[32,768]{1,0:T(8,128)(2,1)S(1)} %mix.6), channel_id=1, source_target_pairs={{0,4},{2,6},{4,0},{6,2},{8,12},{10,14},{12,8},{14,10},{1,5},{3,7},... | collective-permute-start | bytes 147464 | tf_op jit(solution)/shard_map/ppermute | solution.py:169
  25.3 4.1 %collective-permute-start.5 = (bf16[32,640]{1,0:T(8,128)(2,1)S(1)}, bf16[32,640]{1,0:T(8,128)(2,1)S(1)}, u32[]{:S(2)}, u32[]{:S(2)}) collective-permute-start(bf16[32,640]{1,0:T(8,128)(2,1)S(1)} %mix.5), channel_id=1, source_target_pairs={{0,2},{2,0},{4,6},{6,4},{8,10},{10,8},{12,14},{14,12},{1,3},{3,1},... | collective-permute-start | bytes 122888 | tf_op jit(solution)/shard_map/ppermute | solution.py:169

commit v4 on v3

--- a/solution.py
+++ b/solution.py
@@ -268,14 +268,15 @@
             scratch=[pltpu.SemaphoreType.DMA((len(text),))],
         )
 
-        nears = [
-            moved(handed_on([a], text[-1:])[0], 0, 0, turn) if turn else a
-            for turn, a in enumerate(nears)
-        ]
         arrived = [
             moved(message, 0, *mate) for mate, message in zip(mates, messages)
         ]
         crosses = [crosses[0]] + [moved(a, 0, 0, turn) for turn, a in enumerate(crosses) if turn]
+        from_shards = [a for (shift, _), a in zip(mates, arrived) if shift == 0]
+        nears = [
+            moved(handed_on([a], [text[-1], *from_shards])[0], 0, 0, turn) if turn else a
+            for turn, a in enumerate(nears)
+        ]
 
         pieces = []
         if teams > 1:
@@ -285,10 +286,9 @@
                 latest = [moved(piece, 1, 0, 0) for piece in latest]
                 pieces += latest
 
-        cost = pl.CostEstimate(flops=500000000, bytes_accessed=1800000, transcendentals=0)
+        cost = pl.CostEstimate(flops=2000000000, bytes_accessed=7200000, transcendentals=0)
         pieces = handed_on(pieces, cost_estimate=cost) if pieces else pieces
 
-        from_shards = [a for (shift, _), a in zip(mates, arrived) if shift == 0]
         cross_own, *cross_away = call(
             lambda *refs: cross_kernel(shards, *refs),
             "cross",

time: 30.3 us -> 30.4 us (level)
  waiting for transfers between devices: 5.31 us -> 5.9 us
  starting transfers between devices: 15.6 us -> 15.2 us
    ppermute x11, waiting for transfers between devices: 5.31 us -> 5.9 us  [moved(): return lax.ppermute(array, axes, pairs)]
    ppermute x11, starting transfers between devices: 15.6 us -> 15.2 us  [moved(): return lax.ppermute(array, axes, pairs)]
  transfers between devices with their start and end apart: 11 -> 11, of which waited for: 6 -> 4; matrix products, arithmetic and copies ran while one was open for 0% -> 0% of each run, Pallas kernels for 22% -> 22%
where the time goes in v4:
time: 30.4 us; the launch traced here: 30.2 us
  starting transfers between devices  15.2 us (50%)
  Pallas kernels  8.38 us (28%)
  waiting for transfers between devices  5.9 us (19%)
  between operations  0.73 us (2%)
    ppermute x11, starting transfers between devices, moved(): return lax.ppermute(array, axes, pairs)  15.2 us
    pallas_call x15, Pallas kernels, call(): pl.pallas_call(kernel, out_shape=out_shape, in_specs=[in_spec] * len(oper...  8.38 us
    ppermute x11, waiting for transfers between devices, moved(): return lax.ppermute(array, axes, pairs)  5.9 us
  transfers between devices with their start and end apart: 11, of which 4 were waited for; matrix products, arithmetic and copies ran while one was open for 0% of the time, Pallas kernels for 22%

profile of v4, /device:TPU:0, one launch (start us, length us, event | category | flops | bytes accessed | tf_op | source)
XLA Modules:
  0.0 30.2 jit_solution(11339627278440216062)
XLA Ops:
  0.6 1.1 %pack_stale.1 = (bf16[128,640]{1,0:T(8,128)(2,1)S(1)}, bf16[128,640]{1,0:T(8,128)(2,1)S(1)}) custom-call(bf16[1,64,1280]{2,1,0:T(8,128)(2,1)} %refs_0_.2, bf16[1,64,1280]{2,1,0:T(8,128)(2,1)} %refs_1_.2), custom_call_target="tpu_custom_call" | custom-call | tf_op jit(solution)/shard_map/pack_stale/pallas_call | solution.py:106
  1.7 5.1 %collective-permute-start.4 = (bf16[128,640]{1,0:T(8,128)(2,1)S(1)}, bf16[128,640]{1,0:T(8,128)(2,1)S(1)}, u32[]{:S(2)}, u32[]{:S(2)}) collective-permute-start(bf16[128,640]{1,0:T(8,128)(2,1)S(1)} %get-tuple-element.38), channel_id=1, source_target_pairs={{0,12},{2,14},{4,8},{6,10},{8,4},{10,6},{12,0},{14,2},{1,13},{3,15... | collective-permute-start | bytes 491528 | tf_op jit(solution)/shard_map/ppermute | solution.py:169
  6.8 0.0 collective-permute-start.3
  6.8 1.4 %pack.1 = (bf16[96,640]{1,0:T(8,128)(2,1)S(1)}, bf16[32,1280]{1,0:T(8,128)(2,1)S(1)}, bf16[32,1280]{1,0:T(8,128)(2,1)S(1)}, bf16[96,640]{1,0:T(8,128)(2,1)S(1)},...) custom-call(bf16[1,32,2560]{2,1,0:T(8,128)(2,1)} %query.1, ...), custom_call_target="tpu_custom_call" | custom-call | tf_op jit(solution)/shard_map/pack/pallas_call | solution.py:106
  8.2 1.6 %collective-permute-start = (bf16[96,640]{1,0:T(8,128)(2,1)S(1)}, bf16[96,640]{1,0:T(8,128)(2,1)S(1)}, u32[]{:S(2)}, u32[]{:S(2)}) collective-permute-start(bf16[96,640]{1,0:T(8,128)(2,1)S(1)} %get-tuple-element.34), channel_id=1, source_target_pairs={{0,2},{2,0},{4,6},{6,4},{8,10},{10,8},{12,14},{14,12},{1,3},{3,1},... | collective-permute-start | bytes 368648 | tf_op jit(solution)/shard_map/ppermute | solution.py:169
  9.8 0.5 %collective-permute-start.9 = (bf16[32,1280]{1,0:T(8,128)(2,1)S(1)}, bf16[32,1280]{1,0:T(8,128)(2,1)S(1)}, u32[]{:S(2)}, u32[]{:S(2)}) collective-permute-start(bf16[32,1280]{1,0:T(8,128)(2,1)S(1)} %get-tuple-element.59), channel_id=1, source_target_pairs={{0,2},{2,0},{4,6},{6,4},{8,10},{10,8},{12,14},{14,12},{1,3},{3,1},... | collective-permute-start | bytes 245768 | tf_op jit(solution)/shard_map/ppermute | solution.py:169
  10.3 0.6 %collective-permute-start.1 = (bf16[160,640]{1,0:T(8,128)(2,1)S(1)}, bf16[160,640]{1,0:T(8,128)(2,1)S(1)}, u32[]{:S(2)}, u32[]{:S(2)}) collective-permute-start(bf16[160,640]{1,0:T(8,128)(2,1)S(1)} %get-tuple-element.35), channel_id=1, source_target_pairs={{0,4},{2,6},{4,0},{6,2},{8,12},{10,14},{12,8},{14,10},{1,5},{3,7},... | collective-permute-start | bytes 614408 | tf_op jit(solution)/shard_map/ppermute | solution.py:169
  10.9 1.7 %load.1 = (bf16[1,512,1280]{2,1,0:T(8,128)(2,1)S(1)}, bf16[1,512,1280]{2,1,0:T(8,128)(2,1)S(1)}, s32[1,512]{1,0:T(1,128)S(1)}) custom-call(bf16[1,512,1280]{2,1,0:T(8,128)(2,1)} %refs_0_.3, bf16[1,512,1280]{2,1,0:T(8,128)(2,1)} %refs_1_.3, s32[1,512]{1,0:T(1,128)} %refs_2_.1), custom_call_target="tpu_custom_call" | custom-call | tf_op jit(solution)/shard_map/load/pallas_call | solution.py:106
  12.7 2.1 %collective-permute-done.9.refs_1_ = bf16[32,1280]{1,0:T(8,128)(2,1)S(1)} collective-permute-done((bf16[32,1280]{1,0:T(8,128)(2,1)S(1)}, bf16[32,1280]{1,0:T(8,128)(2,1)S(1)}, u32[]{:S(2)}, u32[]{:S(2)}) %collective-permute-start.9) | collective-permute-done | bytes 81952 | tf_op jit(solution)/shard_map/ppermute | solution.py:169
  14.8 1.6 %collective-permute-start.2 = (bf16[32,640]{1,0:T(8,128)(2,1)S(1)}, bf16[32,640]{1,0:T(8,128)(2,1)S(1)}, u32[]{:S(2)}, u32[]{:S(2)}) collective-permute-start(bf16[32,640]{1,0:T(8,128)(2,1)S(1)} %get-tuple-element.36), channel_id=1, source_target_pairs={{0,6},{2,4},{4,2},{6,0},{8,14},{10,12},{12,10},{14,8},{1,7},{3,5},... | collective-permute-start | bytes 122888 | tf_op jit(solution)/shard_map/ppermute | solution.py:169
  16.4 0.0 collective-permute-done.refs_1_.refs_3_.refs_2_.refs_4_.refs_5_
  16.4 0.9 %cross.3 = (bf16[32,1280]{1,0:T(8,128)(2,1)S(1)}, bf16[32,1280]{1,0:T(8,128)(2,1)S(1)}) custom-call(bf16[32,1280]{1,0:T(8,128)(2,1)S(1)} %get-tuple-element.58.refs_0_, bf16[32,1280]{1,0:T(8,128)(2,1)S(1)} %collective-permute-done.9.refs_1_, bf16[1,512,1280]{2,1,0:T(8,128)(2,1)S(1)} %get-tuple-element.60.refs_2_, ...), custom_call_target="tpu_custom_call" | custom-call | tf_op jit(solution)/shard_map/cross/pallas_call | solution.py:106
  17.2 0.6 %collective-permute-start.10 = (bf16[32,1280]{1,0:T(8,128)(2,1)S(1)}, bf16[32,1280]{1,0:T(8,128)(2,1)S(1)}, u32[]{:S(2)}, u32[]{:S(2)}) collective-permute-start(bf16[32,1280]{1,0:T(8,128)(2,1)S(1)} %get-tuple-element.63), channel_id=1, source_target_pairs={{0,2},{2,0},{4,6},{6,4},{8,10},{10,8},{12,14},{14,12},{1,3},{3,1},... | collective-permute-start | bytes 245768 | tf_op jit(solution)/shard_map/ppermute | solution.py:169
  17.8 0.0 collective-permute-done.4.refs_1_
  17.8 1.5 %collective-permute-start.6 = (bf16[64,1280]{1,0:T(8,128)(2,1)S(1)}, bf16[64,1280]{1,0:T(8,128)(2,1)S(1)}, u32[]{:S(2)}, u32[]{:S(2)}) collective-permute-start(bf16[64,1280]{1,0:T(8,128)(2,1)S(1)} %gate.3), channel_id=1, source_target_pairs={{0,2},{2,0},{4,6},{6,4},{8,10},{10,8},{12,14},{14,12},{1,3},{3,1},... | collective-permute-start | bytes 491528 | tf_op jit(solution)/shard_map/ppermute | solution.py:169
  19.3 1.5 %collective-permute-done.3.refs_0_ = bf16[128,640]{1,0:T(8,128)(2,1)S(1)} collective-permute-done((bf16[128,640]{1,0:T(8,128)(2,1)S(1)}, bf16[128,640]{1,0:T(8,128)(2,1)S(1)}, u32[]{:S(2)}, u32[]{:S(2)}) %collective-permute-start.3) | collective-permute-done | bytes 163872 | tf_op jit(solution)/shard_map/ppermute | solution.py:169
  20.8 1.4 %collective-permute-done.2.refs_3_.refs_5_.refs_6_ = bf16[32,640]{1,0:T(8,128)(2,1)S(1)} collective-permute-done((bf16[32,640]{1,0:T(8,128)(2,1)S(1)}, bf16[32,640]{1,0:T(8,128)(2,1)S(1)}, u32[]{:S(2)}, u32[]{:S(2)}) %collective-permute-start.2) | collective-permute-done | bytes 40992 | tf_op jit(solution)/shard_map/ppermute | solution.py:169
  22.2 0.0 collective-permute-done.1.refs_2_.refs_4_.refs_5_
  22.2 0.6 %weights.1 = (bf16[5,32,256]{2,1,0:T(8,128)(2,1)S(1)}, f32[5,32,128]{2,1,0:T(8,128)S(1)}, bf16[5,32,256]{2,1,0:T(8,128)(2,1)S(1)}, f32[5,32,128]{2,1,0:T(8,128)S...) custom-call(bf16[96,640]{1,0:T(8,128)(2,1)S(1)} %get-tuple-element.3, ...), custom_call_target="tpu_custom_call" | custom-call | tf_op jit(solution)/shard_map/weights/pallas_call | solution.py:106
  22.7 0.2 mix.7
  22.9 0.5 %collective-permute-start.8 = (bf16[32,768]{1,0:T(8,128)(2,1)S(1)}, bf16[32,768]{1,0:T(8,128)(2,1)S(1)}, u32[]{:S(2)}, u32[]{:S(2)}) collective-permute-start(bf16[32,768]{1,0:T(8,128)(2,1)S(1)} %mix.7), channel_id=1, source_target_pairs={{0,6},{2,4},{4,2},{6,0},{8,14},{10,12},{12,10},{14,8},{1,7},{3,5},... | collective-permute-start | bytes 147464 | tf_op jit(solution)/shard_map/ppermute | solution.py:169
  23.4 0.2 mix.6
  23.6 1.6 %collective-permute-start.7 = (bf16[32,768]{1,0:T(8,128)(2,1)S(1)}, bf16[32,768]{1,0:T(8,128)(2,1)S(1)}, u32[]{:S(2)}, u32[]{:S(2)}) collective-permute-start(bf16[32,768]{1,0:T(8,128)(2,1)S(1)} %mix.6), channel_id=1, source_target_pairs={{0,4},{2,6},{4,0},{6,2},{8,12},{10,14},{12,8},{14,10},{1,5},{3,7},... | collective-permute-start | bytes 147464 | tf_op jit(solution)/shard_map/ppermute | solution.py:169
  25.2 0.2 mix.5
  25.4 1.6 %collective-permute-start.5 = (bf16[32,640]{1,0:T(8,128)(2,1)S(1)}, bf16[32,640]{1,0:T(8,128)(2,1)S(1)}, u32[]{:S(2)}, u32[]{:S(2)}) collective-permute-start(bf16[32,640]{1,0:T(8,128)(2,1)S(1)} %mix.5), channel_id=1, source_target_pairs={{0,2},{2,0},{4,6},{6,4},{8,10},{10,8},{12,14},{14,12},{1,3},{3,1},... | collective-permute-start | bytes 122888 | tf_op jit(solution)/shard_map/ppermute | solution.py:169
  27.0 0.2 mix.4.refs_0_
  27.2 0.0 collective-permute-done.10.refs_1_
  27.2 0.7 %place_cross.1 = bf16[1,32,2560]{2,1,0:T(8,128)(2,1)} custom-call(bf16[32,1280]{1,0:T(8,128)(2,1)S(1)} %get-tuple-element.62.refs_0_, bf16[32,1280]{1,0:T(8,128)(2,1)S(1)} %collective-permute-done.10.refs_1_), custom_call_target="tpu_custom_call" | custom-call | tf_op jit(solution)/shard_map/place_cross/pallas_call | solution.py:106
  27.9 0.0 collective-permute-done.6.refs_1_
  27.9 0.4 %near.1 = (f32[32,1280]{1,0:T(8,128)S(1)}, f32[10,32,128]{2,1,0:T(8,128)S(1)}) custom-call(bf16[96,1280]{1,0:T(8,128)(2,1)S(1)} %get-tuple-element.45.refs_0_, bf16[64,1280]{1,0:T(8,128)(2,1)S(1)} %collective-permute-done.6.refs_1_), custom_call_target="tpu_custom_call" | custom-call | tf_op jit(solution)/shard_map/near/pallas_call | solution.py:106
  28.3 0.0 collective-permute-done.8.refs_3_
  28.3 0.0 collective-permute-done.7.refs_2_
  28.3 0.2 merge.1
  28.6 0.9 %collective-permute-done.5.refs_1_ = bf16[32,640]{1,0:T(8,128)(2,1)S(1)} collective-permute-done((bf16[32,640]{1,0:T(8,128)(2,1)S(1)}, bf16[32,640]{1,0:T(8,128)(2,1)S(1)}, u32[]{:S(2)}, u32[]{:S(2)}) %collective-permute-start.5) | collective-permute-done | bytes 40992 | tf_op jit(solution)/shard_map/ppermute | solution.py:169
  29.5 0.7 %place_self.1 = bf16[1,32,2560]{2,1,0:T(8,128)(2,1)} custom-call(bf16[32,640]{1,0:T(8,128)(2,1)S(1)} %mix.4.refs_0_, bf16[32,640]{1,0:T(8,128)(2,1)S(1)} %collective-permute-done.5.refs_1_, bf16[32,640]{1,0:T(8,128)(2,1)S(1)} %get-tuple-element.56.refs_2_, bf16[32,640]{1,0:T(8,128)(2,1)S(1)} %get-tuple-element.57.refs_3_), custom_call_target="tpu_custom_call" | custom-call | tf_op jit(solution)/shard_map/place_self/pallas_call | solution.py:106
  (2 shorter events, 0.0 us)
Async XLA Ops:
  1.7 16.1 %collective-permute-start.4 = (bf16[128,640]{1,0:T(8,128)(2,1)S(1)}, bf16[128,640]{1,0:T(8,128)(2,1)S(1)}, u32[]{:S(2)}, u32[]{:S(2)}) collective-permute-start(bf16[128,640]{1,0:T(8,128)(2,1)S(1)} %get-tuple-element.38), channel_id=1, source_target_pairs={{0,12},{2,14},{4,8},{6,10},{8,4},{10,6},{12,0},{14,2},{1,13},{3,15... | collective-permute-start | bytes 491528 | tf_op jit(solution)/shard_map/ppermute | solution.py:169
  6.8 14.0 %collective-permute-start.3 = (bf16[128,640]{1,0:T(8,128)(2,1)S(1)}, bf16[128,640]{1,0:T(8,128)(2,1)S(1)}, u32[]{:S(2)}, u32[]{:S(2)}) collective-permute-start(bf16[128,640]{1,0:T(8,128)(2,1)S(1)} %get-tuple-element.37.refs_4_.refs_6_.refs_7_), channel_id=1, source_target_pairs={{0,8},{2,10},{4,12},{6,14},{8,0},{10,2},{12,4},{14,6},{1,9},{3,11}... | collective-permute-start | bytes 491528 | tf_op jit(solution)/shard_map/ppermute | solution.py:169
  8.2 8.2 %collective-permute-start = (bf16[96,640]{1,0:T(8,128)(2,1)S(1)}, bf16[96,640]{1,0:T(8,128)(2,1)S(1)}, u32[]{:S(2)}, u32[]{:S(2)}) collective-permute-start(bf16[96,640]{1,0:T(8,128)(2,1)S(1)} %get-tuple-element.34), channel_id=1, source_target_pairs={{0,2},{2,0},{4,6},{6,4},{8,10},{10,8},{12,14},{14,12},{1,3},{3,1},... | collective-permute-start | bytes 368648 | tf_op jit(solution)/shard_map/ppermute | solution.py:169
  9.8 5.0 %collective-permute-start.9 = (bf16[32,1280]{1,0:T(8,128)(2,1)S(1)}, bf16[32,1280]{1,0:T(8,128)(2,1)S(1)}, u32[]{:S(2)}, u32[]{:S(2)}) collective-permute-start(bf16[32,1280]{1,0:T(8,128)(2,1)S(1)} %get-tuple-element.59), channel_id=1, source_target_pairs={{0,2},{2,0},{4,6},{6,4},{8,10},{10,8},{12,14},{14,12},{1,3},{3,1},... | collective-permute-start | bytes 245768 | tf_op jit(solution)/shard_map/ppermute | solution.py:169
  10.3 11.9 %collective-permute-start.1 = (bf16[160,640]{1,0:T(8,128)(2,1)S(1)}, bf16[160,640]{1,0:T(8,128)(2,1)S(1)}, u32[]{:S(2)}, u32[]{:S(2)}) collective-permute-start(bf16[160,640]{1,0:T(8,128)(2,1)S(1)} %get-tuple-element.35), channel_id=1, source_target_pairs={{0,4},{2,6},{4,0},{6,2},{8,12},{10,14},{12,8},{14,10},{1,5},{3,7},... | collective-permute-start | bytes 614408 | tf_op jit(solution)/shard_map/ppermute | solution.py:169
  14.8 7.3 %collective-permute-start.2 = (bf16[32,640]{1,0:T(8,128)(2,1)S(1)}, bf16[32,640]{1,0:T(8,128)(2,1)S(1)}, u32[]{:S(2)}, u32[]{:S(2)}) collective-permute-start(bf16[32,640]{1,0:T(8,128)(2,1)S(1)} %get-tuple-element.36), channel_id=1, source_target_pairs={{0,6},{2,4},{4,2},{6,0},{8,14},{10,12},{12,10},{14,8},{1,7},{3,5},... | collective-permute-start | bytes 122888 | tf_op jit(solution)/shard_map/ppermute | solution.py:169
  17.2 9.9 %collective-permute-start.10 = (bf16[32,1280]{1,0:T(8,128)(2,1)S(1)}, bf16[32,1280]{1,0:T(8,128)(2,1)S(1)}, u32[]{:S(2)}, u32[]{:S(2)}) collective-permute-start(bf16[32,1280]{1,0:T(8,128)(2,1)S(1)} %get-tuple-element.63), channel_id=1, source_target_pairs={{0,2},{2,0},{4,6},{6,4},{8,10},{10,8},{12,14},{14,12},{1,3},{3,1},... | collective-permute-start | bytes 245768 | tf_op jit(solution)/shard_map/ppermute | solution.py:169
  17.8 10.0 %collective-permute-start.6 = (bf16[64,1280]{1,0:T(8,128)(2,1)S(1)}, bf16[64,1280]{1,0:T(8,128)(2,1)S(1)}, u32[]{:S(2)}, u32[]{:S(2)}) collective-permute-start(bf16[64,1280]{1,0:T(8,128)(2,1)S(1)} %gate.3), channel_id=1, source_target_pairs={{0,2},{2,0},{4,6},{6,4},{8,10},{10,8},{12,14},{14,12},{1,3},{3,1},... | collective-permute-start | bytes 491528 | tf_op jit(solution)/shard_map/ppermute | solution.py:169
  22.9 5.4 %collective-permute-start.8 = (bf16[32,768]{1,0:T(8,128)(2,1)S(1)}, bf16[32,768]{1,0:T(8,128)(2,1)S(1)}, u32[]{:S(2)}, u32[]{:S(2)}) collective-permute-start(bf16[32,768]{1,0:T(8,128)(2,1)S(1)} %mix.7), channel_id=1, source_target_pairs={{0,6},{2,4},{4,2},{6,0},{8,14},{10,12},{12,10},{14,8},{1,7},{3,5},... | collective-permute-start | bytes 147464 | tf_op jit(solution)/shard_map/ppermute | solution.py:169
  23.6 4.7 %collective-permute-start.7 = (bf16[32,768]{1,0:T(8,128)(2,1)S(1)}, bf16[32,768]{1,0:T(8,128)(2,1)S(1)}, u32[]{:S(2)}, u32[]{:S(2)}) collective-permute-start(bf16[32,768]{1,0:T(8,128)(2,1)S(1)} %mix.6), channel_id=1, source_target_pairs={{0,4},{2,6},{4,0},{6,2},{8,12},{10,14},{12,8},{14,10},{1,5},{3,7},... | collective-permute-start | bytes 147464 | tf_op jit(solution)/shard_map/ppermute | solution.py:169
  25.4 4.1 %collective-permute-start.5 = (bf16[32,640]{1,0:T(8,128)(2,1)S(1)}, bf16[32,640]{1,0:T(8,128)(2,1)S(1)}, u32[]{:S(2)}, u32[]{:S(2)}) collective-permute-start(bf16[32,640]{1,0:T(8,128)(2,1)S(1)} %mix.5), channel_id=1, source_target_pairs={{0,2},{2,0},{4,6},{6,4},{8,10},{10,8},{12,14},{14,12},{1,3},{3,1},... | collective-permute-start | bytes 122888 | tf_op jit(solution)/shard_map/ppermute | solution.py:169

commit v5 on v3

--- a/solution.py
+++ b/solution.py
@@ -412,9 +412,17 @@
                 mixed = weighted(weights_ref[head], jnp.concatenate(values, axis=0))
                 target[:, lanes] = (mixed * shares_ref[head]).astype(target.dtype)
 
-        def mate_mix_kernel(shift, weights_ref, shares_ref, logs_ref, *refs):
-            mix_kernel(shift, weights_ref, shares_ref, *refs[:-1], refs[-1].at[:, pl.ds(0, width)])
-            refs[-1][:, width:] = logs_ref[...]
+        def mate_mix_kernel(shift, *refs):
+            parts_in, sources, targets = refs[: 3 * shards], refs[3 * shards : -shards], refs[-shards:]
+            for head in range(share_heads):
+                lanes = head_lanes(head)
+                values = jnp.concatenate(stale_of(sources, shift, 1, lanes), axis=0)
+                for turn, target in enumerate(targets):
+                    weights_ref, shares_ref = parts_in[3 * turn : 3 * turn + 2]
+                    mixed = weighted(weights_ref[head], values) * shares_ref[head]
+                    target[:, lanes] = mixed.astype(target.dtype)
+            for turn, target in enumerate(targets):
+                target[:, width:] = parts_in[3 * turn + 2][...]
 
         def merge_kernel(*refs):
             (sums_ref, logs_ref), refs = refs[:2], refs[2:]
@@ -445,18 +453,32 @@
         )
 
         def mixed(spot):
-            pair, shift = parts[2 * spot : 2 * spot + 2], spots[spot][0]
-            if shift == 0:
-                kernel, shape = mix_kernel, (rows, width)
-            else:
-                kernel, shape = mate_mix_kernel, (rows, width + HD)
-                pair = (*pair, parts[2 * len(spots) + over_patch.index(spots[spot])])
             return call(
-                lambda *refs: kernel(shift, *refs), "mix", pltpu.VMEM(shape, kind), (*pair, *sources)
+                lambda *refs: mix_kernel(0, *refs),
+                "mix",
+                pltpu.VMEM((rows, width), kind),
+                (*parts[2 * spot : 2 * spot + 2], *sources),
             )
 
+        def mate_mixed(shift):
+            operands = []
+            for turn in range(shards):
+                spot = spots.index((shift, turn))
+                logs = parts[2 * len(spots) + over_patch.index((shift, turn))]
+                operands += [*parts[2 * spot : 2 * spot + 2], logs]
+            made = call(
+                lambda *refs: mate_mix_kernel(shift, *refs),
+                "mix_mate",
+                [pltpu.VMEM((rows, width + HD), kind)] * shards,
+                (*operands, *sources),
+            )
+            return {(shift, turn): a for turn, a in enumerate(made)}
+
+        ready = {}
+        for shift in range(1, share):
+            ready.update(mate_mixed(shift))
         back = [
-            moved(mixed(index), 0, -shift, -turn)
+            moved(ready[shift, turn] if shift else mixed(index), 0, -shift, -turn)
             for index, (shift, turn) in enumerate(spots)
             if index > 0
         ]

time: 30.3 us -> 30.2 us (level)
    pallas_call x15 -> x14, Pallas kernels: 8.41 us -> 8.31 us  [call(): pl.pallas_call(kernel, out_shape=out_shape, in_specs=[in_spec] * len(oper...]
where the time goes in v5:
time: 30.2 us; the launch traced here: 29.9 us
  starting transfers between devices  15.6 us (52%)
  Pallas kernels  8.31 us (28%)
  waiting for transfers between devices  5.31 us (18%)
  between operations  0.73 us (2%)
    ppermute x11, starting transfers between devices, moved(): return lax.ppermute(array, axes, pairs)  15.6 us
    pallas_call x14, Pallas kernels, call(): pl.pallas_call(kernel, out_shape=out_shape, in_specs=[in_spec] * len(oper...  8.31 us
    ppermute x11, waiting for transfers between devices, moved(): return lax.ppermute(array, axes, pairs)  5.31 us
  transfers between devices with their start and end apart: 11, of which 6 were waited for; matrix products, arithmetic and copies ran while one was open for 0% of the time, Pallas kernels for 22%

profile of v5, /device:TPU:0, one launch (start us, length us, event | category | flops | bytes accessed | tf_op | source)
XLA Modules:
  0.0 29.9 jit_solution(3982326975939853868)
XLA Ops:
  0.6 1.1 %pack_stale.1 = (bf16[128,640]{1,0:T(8,128)(2,1)S(1)}, bf16[128,640]{1,0:T(8,128)(2,1)S(1)}) custom-call(bf16[1,64,1280]{2,1,0:T(8,128)(2,1)} %refs_0_.2, bf16[1,64,1280]{2,1,0:T(8,128)(2,1)} %refs_1_.2), custom_call_target="tpu_custom_call" | custom-call | tf_op jit(solution)/shard_map/pack_stale/pallas_call | solution.py:106
  1.7 5.1 %collective-permute-start.4 = (bf16[128,640]{1,0:T(8,128)(2,1)S(1)}, bf16[128,640]{1,0:T(8,128)(2,1)S(1)}, u32[]{:S(2)}, u32[]{:S(2)}) collective-permute-start(bf16[128,640]{1,0:T(8,128)(2,1)S(1)} %get-tuple-element.40), channel_id=1, source_target_pairs={{0,12},{2,14},{4,8},{6,10},{8,4},{10,6},{12,0},{14,2},{1,13},{3,15... | collective-permute-start | bytes 491528 | tf_op jit(solution)/shard_map/ppermute | solution.py:169
  6.8 0.0 collective-permute-start.3
  6.8 1.4 %pack.1 = (bf16[96,640]{1,0:T(8,128)(2,1)S(1)}, bf16[32,1280]{1,0:T(8,128)(2,1)S(1)}, bf16[32,1280]{1,0:T(8,128)(2,1)S(1)}, bf16[96,640]{1,0:T(8,128)(2,1)S(1)},...) custom-call(bf16[1,32,2560]{2,1,0:T(8,128)(2,1)} %query.1, ...), custom_call_target="tpu_custom_call" | custom-call | tf_op jit(solution)/shard_map/pack/pallas_call | solution.py:106
  8.2 0.7 %collective-permute-start.1 = (bf16[160,640]{1,0:T(8,128)(2,1)S(1)}, bf16[160,640]{1,0:T(8,128)(2,1)S(1)}, u32[]{:S(2)}, u32[]{:S(2)}) collective-permute-start(bf16[160,640]{1,0:T(8,128)(2,1)S(1)} %get-tuple-element.37), channel_id=1, source_target_pairs={{0,4},{2,6},{4,0},{6,2},{8,12},{10,14},{12,8},{14,10},{1,5},{3,7},... | collective-permute-start | bytes 614408 | tf_op jit(solution)/shard_map/ppermute | solution.py:169
  8.9 1.6 %collective-permute-start.9 = (bf16[32,1280]{1,0:T(8,128)(2,1)S(1)}, bf16[32,1280]{1,0:T(8,128)(2,1)S(1)}, u32[]{:S(2)}, u32[]{:S(2)}) collective-permute-start(bf16[32,1280]{1,0:T(8,128)(2,1)S(1)} %get-tuple-element.63), channel_id=1, source_target_pairs={{0,2},{2,0},{4,6},{6,4},{8,10},{10,8},{12,14},{14,12},{1,3},{3,1},... | collective-permute-start | bytes 245768 | tf_op jit(solution)/shard_map/ppermute | solution.py:169
  10.6 0.4 %collective-permute-start = (bf16[96,640]{1,0:T(8,128)(2,1)S(1)}, bf16[96,640]{1,0:T(8,128)(2,1)S(1)}, u32[]{:S(2)}, u32[]{:S(2)}) collective-permute-start(bf16[96,640]{1,0:T(8,128)(2,1)S(1)} %get-tuple-element.36), channel_id=1, source_target_pairs={{0,2},{2,0},{4,6},{6,4},{8,10},{10,8},{12,14},{14,12},{1,3},{3,1},... | collective-permute-start | bytes 368648 | tf_op jit(solution)/shard_map/ppermute | solution.py:169
  10.9 1.7 %load.1 = (bf16[1,512,1280]{2,1,0:T(8,128)(2,1)S(1)}, bf16[1,512,1280]{2,1,0:T(8,128)(2,1)S(1)}, s32[1,512]{1,0:T(1,128)S(1)}) custom-call(bf16[1,512,1280]{2,1,0:T(8,128)(2,1)} %refs_0_.3, bf16[1,512,1280]{2,1,0:T(8,128)(2,1)} %refs_1_.3, s32[1,512]{1,0:T(1,128)} %refs_2_.1), custom_call_target="tpu_custom_call" | custom-call | tf_op jit(solution)/shard_map/load/pallas_call | solution.py:106
  12.7 1.5 %collective-permute-done.9.refs_1_ = bf16[32,1280]{1,0:T(8,128)(2,1)S(1)} collective-permute-done((bf16[32,1280]{1,0:T(8,128)(2,1)S(1)}, bf16[32,1280]{1,0:T(8,128)(2,1)S(1)}, u32[]{:S(2)}, u32[]{:S(2)}) %collective-permute-start.9) | collective-permute-done | bytes 81952 | tf_op jit(solution)/shard_map/ppermute | solution.py:169
  14.2 1.2 %collective-permute-start.6 = (bf16[64,1280]{1,0:T(8,128)(2,1)S(1)}, bf16[64,1280]{1,0:T(8,128)(2,1)S(1)}, u32[]{:S(2)}, u32[]{:S(2)}) collective-permute-start(bf16[64,1280]{1,0:T(8,128)(2,1)S(1)} %gate.3), channel_id=1, source_target_pairs={{0,2},{2,0},{4,6},{6,4},{8,10},{10,8},{12,14},{14,12},{1,3},{3,1},... | collective-permute-start | bytes 491528 | tf_op jit(solution)/shard_map/ppermute | solution.py:169
  15.3 1.2 %collective-permute-done.refs_1_.refs_3_.refs_7_.refs_5_ = bf16[96,640]{1,0:T(8,128)(2,1)S(1)} collective-permute-done((bf16[96,640]{1,0:T(8,128)(2,1)S(1)}, bf16[96,640]{1,0:T(8,128)(2,1)S(1)}, u32[]{:S(2)}, u32[]{:S(2)}) %collective-permute-start) | collective-permute-done | bytes 122912 | tf_op jit(solution)/shard_map/ppermute | solution.py:169
  16.6 1.6 %collective-permute-start.2 = (bf16[32,640]{1,0:T(8,128)(2,1)S(1)}, bf16[32,640]{1,0:T(8,128)(2,1)S(1)}, u32[]{:S(2)}, u32[]{:S(2)}) collective-permute-start(bf16[32,640]{1,0:T(8,128)(2,1)S(1)} %get-tuple-element.38), channel_id=1, source_target_pairs={{0,6},{2,4},{4,2},{6,0},{8,14},{10,12},{12,10},{14,8},{1,7},{3,5},... | collective-permute-start | bytes 122888 | tf_op jit(solution)/shard_map/ppermute | solution.py:169
  18.2 0.9 %cross.3 = (bf16[32,1280]{1,0:T(8,128)(2,1)S(1)}, bf16[32,1280]{1,0:T(8,128)(2,1)S(1)}) custom-call(bf16[32,1280]{1,0:T(8,128)(2,1)S(1)} %get-tuple-element.62.refs_0_, bf16[32,1280]{1,0:T(8,128)(2,1)S(1)} %collective-permute-done.9.refs_1_, bf16[1,512,1280]{2,1,0:T(8,128)(2,1)S(1)} %get-tuple-element.64.refs_2_, ...), custom_call_target="tpu_custom_call" | custom-call | tf_op jit(solution)/shard_map/cross/pallas_call | solution.py:106
  19.1 0.0 collective-permute-done.4.refs_1_
  19.1 1.3 %collective-permute-start.10 = (bf16[32,1280]{1,0:T(8,128)(2,1)S(1)}, bf16[32,1280]{1,0:T(8,128)(2,1)S(1)}, u32[]{:S(2)}, u32[]{:S(2)}) collective-permute-start(bf16[32,1280]{1,0:T(8,128)(2,1)S(1)} %get-tuple-element.67), channel_id=1, source_target_pairs={{0,2},{2,0},{4,6},{6,4},{8,10},{10,8},{12,14},{14,12},{1,3},{3,1},... | collective-permute-start | bytes 245768 | tf_op jit(solution)/shard_map/ppermute | solution.py:169
  20.4 0.3 %collective-permute-done.3.refs_0_ = bf16[128,640]{1,0:T(8,128)(2,1)S(1)} collective-permute-done((bf16[128,640]{1,0:T(8,128)(2,1)S(1)}, bf16[128,640]{1,0:T(8,128)(2,1)S(1)}, u32[]{:S(2)}, u32[]{:S(2)}) %collective-permute-start.3) | collective-permute-done | bytes 163872 | tf_op jit(solution)/shard_map/ppermute | solution.py:169
  20.7 1.3 %collective-permute-done.2.refs_3_.refs_5_.refs_9_ = bf16[32,640]{1,0:T(8,128)(2,1)S(1)} collective-permute-done((bf16[32,640]{1,0:T(8,128)(2,1)S(1)}, bf16[32,640]{1,0:T(8,128)(2,1)S(1)}, u32[]{:S(2)}, u32[]{:S(2)}) %collective-permute-start.2) | collective-permute-done | bytes 40992 | tf_op jit(solution)/shard_map/ppermute | solution.py:169
  22.1 0.0 collective-permute-done.1.refs_2_.refs_4_.refs_8_
  22.1 0.6 %weights.1 = (bf16[5,32,256]{2,1,0:T(8,128)(2,1)S(1)}, f32[5,32,128]{2,1,0:T(8,128)S(1)}, bf16[5,32,256]{2,1,0:T(8,128)(2,1)S(1)}, f32[5,32,128]{2,1,0:T(8,128)S...) custom-call(bf16[96,640]{1,0:T(8,128)(2,1)S(1)} %get-tuple-element.3, ...), custom_call_target="tpu_custom_call" | custom-call | tf_op jit(solution)/shard_map/weights/pallas_call | solution.py:106
  22.6 0.3 mix_mate.1
  22.9 0.9 %collective-permute-start.7 = (bf16[32,768]{1,0:T(8,128)(2,1)S(1)}, bf16[32,768]{1,0:T(8,128)(2,1)S(1)}, u32[]{:S(2)}, u32[]{:S(2)}) collective-permute-start(bf16[32,768]{1,0:T(8,128)(2,1)S(1)} %get-tuple-element.58), channel_id=1, source_target_pairs={{0,4},{2,6},{4,0},{6,2},{8,12},{10,14},{12,8},{14,10},{1,5},{3,7},... | collective-permute-start | bytes 147464 | tf_op jit(solution)/shard_map/ppermute | solution.py:169
  23.8 1.2 %collective-permute-start.8 = (bf16[32,768]{1,0:T(8,128)(2,1)S(1)}, bf16[32,768]{1,0:T(8,128)(2,1)S(1)}, u32[]{:S(2)}, u32[]{:S(2)}) collective-permute-start(bf16[32,768]{1,0:T(8,128)(2,1)S(1)} %get-tuple-element.59), channel_id=1, source_target_pairs={{0,6},{2,4},{4,2},{6,0},{8,14},{10,12},{12,10},{14,8},{1,7},{3,5},... | collective-permute-start | bytes 147464 | tf_op jit(solution)/shard_map/ppermute | solution.py:169
  25.0 0.2 mix.3
  25.2 1.6 %collective-permute-start.5 = (bf16[32,640]{1,0:T(8,128)(2,1)S(1)}, bf16[32,640]{1,0:T(8,128)(2,1)S(1)}, u32[]{:S(2)}, u32[]{:S(2)}) collective-permute-start(bf16[32,640]{1,0:T(8,128)(2,1)S(1)} %mix.3), channel_id=1, source_target_pairs={{0,2},{2,0},{4,6},{6,4},{8,10},{10,8},{12,14},{14,12},{1,3},{3,1},... | collective-permute-start | bytes 122888 | tf_op jit(solution)/shard_map/ppermute | solution.py:169
  26.7 0.0 collective-permute-done.6.refs_1_
  26.7 0.4 %near.1 = (f32[32,1280]{1,0:T(8,128)S(1)}, f32[10,32,128]{2,1,0:T(8,128)S(1)}) custom-call(bf16[96,1280]{1,0:T(8,128)(2,1)S(1)} %get-tuple-element.47.refs_0_, bf16[64,1280]{1,0:T(8,128)(2,1)S(1)} %collective-permute-done.6.refs_1_), custom_call_target="tpu_custom_call" | custom-call | tf_op jit(solution)/shard_map/near/pallas_call | solution.py:106
  27.1 0.2 mix.2.refs_0_
  27.3 0.0 collective-permute-done.10.refs_1_
  27.3 0.7 %place_cross.1 = bf16[1,32,2560]{2,1,0:T(8,128)(2,1)} custom-call(bf16[32,1280]{1,0:T(8,128)(2,1)S(1)} %get-tuple-element.66.refs_0_, bf16[32,1280]{1,0:T(8,128)(2,1)S(1)} %collective-permute-done.10.refs_1_), custom_call_target="tpu_custom_call" | custom-call | tf_op jit(solution)/shard_map/place_cross/pallas_call | solution.py:106
  28.0 0.0 collective-permute-done.7.refs_2_
  28.1 0.7 %collective-permute-done.8.refs_3_ = bf16[32,768]{1,0:T(8,128)(2,1)S(1)} collective-permute-done((bf16[32,768]{1,0:T(8,128)(2,1)S(1)}, bf16[32,768]{1,0:T(8,128)(2,1)S(1)}, u32[]{:S(2)}, u32[]{:S(2)}) %collective-permute-start.8) | collective-permute-done | bytes 49184 | tf_op jit(solution)/shard_map/ppermute | solution.py:169
  28.8 0.2 merge.1
  29.0 0.2 collective-permute-done.5.refs_1_
  29.2 0.7 %place_self.1 = bf16[1,32,2560]{2,1,0:T(8,128)(2,1)} custom-call(bf16[32,640]{1,0:T(8,128)(2,1)S(1)} %mix.2.refs_0_, bf16[32,640]{1,0:T(8,128)(2,1)S(1)} %collective-permute-done.5.refs_1_, bf16[32,640]{1,0:T(8,128)(2,1)S(1)} %get-tuple-element.60.refs_2_, bf16[32,640]{1,0:T(8,128)(2,1)S(1)} %get-tuple-element.61.refs_3_), custom_call_target="tpu_custom_call" | custom-call | tf_op jit(solution)/shard_map/place_self/pallas_call | solution.py:106
  (2 shorter events, 0.0 us)
Async XLA Ops:
  1.7 17.4 %collective-permute-start.4 = (bf16[128,640]{1,0:T(8,128)(2,1)S(1)}, bf16[128,640]{1,0:T(8,128)(2,1)S(1)}, u32[]{:S(2)}, u32[]{:S(2)}) collective-permute-start(bf16[128,640]{1,0:T(8,128)(2,1)S(1)} %get-tuple-element.40), channel_id=1, source_target_pairs={{0,12},{2,14},{4,8},{6,10},{8,4},{10,6},{12,0},{14,2},{1,13},{3,15... | collective-permute-start | bytes 491528 | tf_op jit(solution)/shard_map/ppermute | solution.py:169
  6.8 13.9 %collective-permute-start.3 = (bf16[128,640]{1,0:T(8,128)(2,1)S(1)}, bf16[128,640]{1,0:T(8,128)(2,1)S(1)}, u32[]{:S(2)}, u32[]{:S(2)}) collective-permute-start(bf16[128,640]{1,0:T(8,128)(2,1)S(1)} %get-tuple-element.39.refs_4_.refs_6_.refs_10_), channel_id=1, source_target_pairs={{0,8},{2,10},{4,12},{6,14},{8,0},{10,2},{12,4},{14,6},{1,9},{3,11}... | collective-permute-start | bytes 491528 | tf_op jit(solution)/shard_map/ppermute | solution.py:169
  8.2 13.8 %collective-permute-start.1 = (bf16[160,640]{1,0:T(8,128)(2,1)S(1)}, bf16[160,640]{1,0:T(8,128)(2,1)S(1)}, u32[]{:S(2)}, u32[]{:S(2)}) collective-permute-start(bf16[160,640]{1,0:T(8,128)(2,1)S(1)} %get-tuple-element.37), channel_id=1, source_target_pairs={{0,4},{2,6},{4,0},{6,2},{8,12},{10,14},{12,8},{14,10},{1,5},{3,7},... | collective-permute-start | bytes 614408 | tf_op jit(solution)/shard_map/ppermute | solution.py:169
  8.9 5.2 %collective-permute-start.9 = (bf16[32,1280]{1,0:T(8,128)(2,1)S(1)}, bf16[32,1280]{1,0:T(8,128)(2,1)S(1)}, u32[]{:S(2)}, u32[]{:S(2)}) collective-permute-start(bf16[32,1280]{1,0:T(8,128)(2,1)S(1)} %get-tuple-element.63), channel_id=1, source_target_pairs={{0,2},{2,0},{4,6},{6,4},{8,10},{10,8},{12,14},{14,12},{1,3},{3,1},... | collective-permute-start | bytes 245768 | tf_op jit(solution)/shard_map/ppermute | solution.py:169
  10.6 6.0 %collective-permute-start = (bf16[96,640]{1,0:T(8,128)(2,1)S(1)}, bf16[96,640]{1,0:T(8,128)(2,1)S(1)}, u32[]{:S(2)}, u32[]{:S(2)}) collective-permute-start(bf16[96,640]{1,0:T(8,128)(2,1)S(1)} %get-tuple-element.36), channel_id=1, source_target_pairs={{0,2},{2,0},{4,6},{6,4},{8,10},{10,8},{12,14},{14,12},{1,3},{3,1},... | collective-permute-start | bytes 368648 | tf_op jit(solution)/shard_map/ppermute | solution.py:169
  14.2 12.6 %collective-permute-start.6 = (bf16[64,1280]{1,0:T(8,128)(2,1)S(1)}, bf16[64,1280]{1,0:T(8,128)(2,1)S(1)}, u32[]{:S(2)}, u32[]{:S(2)}) collective-permute-start(bf16[64,1280]{1,0:T(8,128)(2,1)S(1)} %gate.3), channel_id=1, source_target_pairs={{0,2},{2,0},{4,6},{6,4},{8,10},{10,8},{12,14},{14,12},{1,3},{3,1},... | collective-permute-start | bytes 491528 | tf_op jit(solution)/shard_map/ppermute | solution.py:169
  16.6 5.5 %collective-permute-start.2 = (bf16[32,640]{1,0:T(8,128)(2,1)S(1)}, bf16[32,640]{1,0:T(8,128)(2,1)S(1)}, u32[]{:S(2)}, u32[]{:S(2)}) collective-permute-start(bf16[32,640]{1,0:T(8,128)(2,1)S(1)} %get-tuple-element.38), channel_id=1, source_target_pairs={{0,6},{2,4},{4,2},{6,0},{8,14},{10,12},{12,10},{14,8},{1,7},{3,5},... | collective-permute-start | bytes 122888 | tf_op jit(solution)/shard_map/ppermute | solution.py:169
  19.1 8.2 %collective-permute-start.10 = (bf16[32,1280]{1,0:T(8,128)(2,1)S(1)}, bf16[32,1280]{1,0:T(8,128)(2,1)S(1)}, u32[]{:S(2)}, u32[]{:S(2)}) collective-permute-start(bf16[32,1280]{1,0:T(8,128)(2,1)S(1)} %get-tuple-element.67), channel_id=1, source_target_pairs={{0,2},{2,0},{4,6},{6,4},{8,10},{10,8},{12,14},{14,12},{1,3},{3,1},... | collective-permute-start | bytes 245768 | tf_op jit(solution)/shard_map/ppermute | solution.py:169
  22.9 5.1 %collective-permute-start.7 = (bf16[32,768]{1,0:T(8,128)(2,1)S(1)}, bf16[32,768]{1,0:T(8,128)(2,1)S(1)}, u32[]{:S(2)}, u32[]{:S(2)}) collective-permute-start(bf16[32,768]{1,0:T(8,128)(2,1)S(1)} %get-tuple-element.58), channel_id=1, source_target_pairs={{0,4},{2,6},{4,0},{6,2},{8,12},{10,14},{12,8},{14,10},{1,5},{3,7},... | collective-permute-start | bytes 147464 | tf_op jit(solution)/shard_map/ppermute | solution.py:169
  23.8 5.0 %collective-permute-start.8 = (bf16[32,768]{1,0:T(8,128)(2,1)S(1)}, bf16[32,768]{1,0:T(8,128)(2,1)S(1)}, u32[]{:S(2)}, u32[]{:S(2)}) collective-permute-start(bf16[32,768]{1,0:T(8,128)(2,1)S(1)} %get-tuple-element.59), channel_id=1, source_target_pairs={{0,6},{2,4},{4,2},{6,0},{8,14},{10,12},{12,10},{14,8},{1,7},{3,5},... | collective-permute-start | bytes 147464 | tf_op jit(solution)/shard_map/ppermute | solution.py:169
  25.2 4.1 %collective-permute-start.5 = (bf16[32,640]{1,0:T(8,128)(2,1)S(1)}, bf16[32,640]{1,0:T(8,128)(2,1)S(1)}, u32[]{:S(2)}, u32[]{:S(2)}) collective-permute-start(bf16[32,640]{1,0:T(8,128)(2,1)S(1)} %mix.3), channel_id=1, source_target_pairs={{0,2},{2,0},{4,6},{6,4},{8,10},{10,8},{12,14},{14,12},{1,3},{3,1},... | collective-permute-start | bytes 122888 | tf_op jit(solution)/shard_map/ppermute | solution.py:169
